TPU v7x, 512 devices: a whole 4x4x16 slice. The times are simulated.
512 devices in a mesh: gx: 32 (over z_hi, x, core), gy: 16 (over y, z_lo).
Axes of the slice: x: 4, y: 4, z: 16 (z_hi: 4, z_lo: 4; z = z_hi * 4 + z_lo), core: 2. Of those that a mesh axis runs over, the one named last changes fastest.
Arguments:
- feats: bfloat16 [32, 16, 2, 128, 512], P('gx', 'gy'), may hold values from -12 to 12
- w_query: bfloat16 [512, 512], replicated, may hold values from -1 to 1
- w_key: bfloat16 [512, 512], replicated, may hold values from -1 to 1
- w_value: bfloat16 [512, 512], replicated, may hold values from -0.25 to 0.25
- out_grad: bfloat16 [32, 16, 2, 128, 512], P('gx', 'gy'), may hold values from -6 to 6
- patch_count: int32 [32, 16], P('gx', 'gy'), may hold values from 1 to 2
- point_count: int32 [32, 16, 2], P('gx', 'gy'), may hold values from 32 to 128
- neighbours: int32 [32, 16, 2, 3], P('gx', 'gy'), may hold values from 0 to 9, as said below
- neighbour_points: int32 [32, 16, 2, 3], P('gx', 'gy'), may hold values from 32 to 128, as said below
Outputs:
- mixed: bfloat16 [32, 16, 2, 128, 512], P('gx', 'gy')
- feat_grad: bfloat16 [32, 16, 2, 128, 512], P('gx', 'gy')
- grad_query: bfloat16 [512, 512], replicated
- grad_key: bfloat16 [512, 512], replicated
- grad_value: bfloat16 [512, 512], replicated
Inputs may be any that keep to these rules, and one draw needn't show every extreme that they name: `neighbour_points`: equal to point_count of the patch that the same entry of neighbours names.
All inputs are finite; a program needn't handle non-finite values.
Results may differ from a plain program's by a relative error of at most 0.015.
Values may be sent and summed in bfloat16 or wider, within the bound.
A program may use at most 64 MiB of HBM per device.

v0:
```python
import jax
import jax.numpy as jnp
from jax import lax
from jax.sharding import PartitionSpec as P

HEADS = 8


def with_halo(x, sides, width):
    for axis, dim in sides:
        peers, length = (lax.axis_size(axis), x.shape[dim])
        up = [(i, (i + 1) % peers) for i in range(peers - 1)]
        down = [(j, i) for i, j in up]
        last = lax.slice_in_dim(x, length - width, length, axis=dim)
        initial = lax.slice_in_dim(x, 0, width, axis=dim)
        before = lax.ppermute(last, axis, up)
        after = lax.ppermute(initial, axis, down)
        x = jnp.concatenate([before, x, after], axis=dim)
    return x


def passed_along(value, axis, steps):
    count = lax.axis_size(axis)
    initial, last = (max(0, -steps), min(count, count - steps))
    return lax.ppermute(value, axis, [(source, source + steps) for source in range(initial, last)])


def one_slot(items):
    qq, keys, key_valid, live, grads = items
    points, width = qq.shape
    head_dim = width // HEADS
    scale = head_dim ** (-0.5)
    kk = keys[:, :width].reshape(-1, HEADS, head_dim)
    vv = keys[:, width:].reshape(-1, HEADS, head_dim)
    qh = qq.reshape(points, HEADS, head_dim)
    scores = jnp.einsum("qhd,khd->hqk", qh, kk, preferred_element_type=jnp.float32) * scale
    scores = jnp.where(key_valid[None, None, :], scores, -1e30)
    top = jnp.max(scores, axis=-1, keepdims=True)
    expo = jnp.exp(scores - top)
    probs = expo / jnp.sum(expo, axis=-1, keepdims=True)
    probs_b = probs.astype(jnp.bfloat16)
    mixed = jnp.einsum("hqk,khd->qhd", probs_b, vv, preferred_element_type=jnp.float32)
    alive = live[:, None, None]
    out = jnp.where(alive, mixed, 0.0).astype(jnp.bfloat16).reshape(points, width)
    gradh = grads.reshape(points, HEADS, head_dim)
    dout = jnp.where(alive, gradh, jnp.zeros_like(gradh))
    dprob = jnp.einsum("qhd,khd->hqk", dout, vv, preferred_element_type=jnp.float32)
    inner = jnp.sum(probs * dprob, axis=-1, keepdims=True)
    dscore = (probs * (dprob - inner) * scale).astype(jnp.bfloat16)
    dquery = jnp.einsum("hqk,khd->qhd", dscore, kk, preferred_element_type=jnp.float32)
    dquery = dquery.astype(jnp.bfloat16).reshape(points, width)
    dkey = jnp.einsum("hqk,qhd->khd", dscore, qh, preferred_element_type=jnp.float32)
    dval = jnp.einsum("hqk,qhd->khd", probs_b, dout, preferred_element_type=jnp.float32)
    contrib = jnp.concatenate(
        [dkey.reshape(-1, points, width), dval.reshape(-1, points, width)], axis=-1
    )
    return (out, dquery, contrib)


def attend(query, table, codes, key_len, q_valid, grad_out):
    slots, points, width = query.shape
    keys = table.reshape(-1, points, 2 * width)[codes].reshape(slots, -1, 2 * width)
    key_valid = (jnp.arange(points, dtype=jnp.int32)[None, None, :] < key_len[:, :, None]).reshape(
        slots, -1
    )
    out, dquery, contrib = lax.map(one_slot, (query, keys, key_valid, q_valid, grad_out))
    contrib = contrib.reshape(-1, points * 2 * width)
    onehot = (jnp.arange(5 * slots, dtype=jnp.int32)[:, None] == codes.reshape(1, -1)).astype(
        jnp.float32
    )
    partial_value = jnp.dot(
        onehot, contrib, precision=lax.Precision.HIGHEST, preferred_element_type=jnp.float32
    )
    partial_value = partial_value.astype(jnp.bfloat16).reshape(5, slots, points, 2 * width)
    return (out, dquery, partial_value)


def faces_of(wide):
    return jnp.stack([wide[0, 1], wide[2, 1], wide[1, 0], wide[1, 2]])


def project(rows, weight):
    return jnp.dot(rows, weight, preferred_element_type=jnp.float32).astype(jnp.bfloat16)


def body(
    feats, w_query, w_key, w_value, out_grad, patch_count, point_count, neighbours, neighbour_points
):
    slots, points, width = (feats.shape[2], feats.shape[3], feats.shape[4])
    flat = feats.reshape(-1, width)
    query = project(flat, w_query).reshape(slots, points, width)
    keyval = jnp.concatenate([project(flat, w_key), project(flat, w_value)], axis=-1).reshape(
        slots, points, 2 * width
    )
    wide = with_halo(keyval[None, None], (("gx", 0), ("gy", 1)), 1)
    faces = faces_of(wide)
    table = jnp.concatenate([keyval[None], faces], axis=0)
    codes = jnp.concatenate([jnp.arange(slots, dtype=jnp.int32)[:, None], neighbours[0, 0]], axis=1)
    counts = point_count[0, 0]
    key_len = jnp.concatenate([counts[:, None], neighbour_points[0, 0]], axis=1)
    q_valid = (jnp.arange(slots, dtype=jnp.int32)[:, None] < patch_count[0, 0]) & (
        jnp.arange(points, dtype=jnp.int32)[None, :] < counts[:, None]
    )
    out, dquery, partial_value = attend(query, table, codes, key_len, q_valid, out_grad[0, 0])
    total = partial_value[0].astype(jnp.float32)
    for shift_by, place in ((-1, 1), (1, 2)):
        total = total + passed_along(partial_value[place], "gx", shift_by).astype(jnp.float32)
    for shift_by, place in ((-1, 3), (1, 4)):
        total = total + passed_along(partial_value[place], "gy", shift_by).astype(jnp.float32)
    grads = total.astype(jnp.bfloat16)
    dq = dquery.reshape(-1, width)
    dk = grads[..., :width].reshape(-1, width)
    dv = grads[..., width:].reshape(-1, width)
    back = (((1,), (1,)), ((), ()))
    feat_grad = (
        lax.dot_general(dq, w_query, back, preferred_element_type=jnp.float32)
        + lax.dot_general(dk, w_key, back, preferred_element_type=jnp.float32)
        + lax.dot_general(dv, w_value, back, preferred_element_type=jnp.float32)
    )
    feat_grad = feat_grad.astype(jnp.bfloat16).reshape(feats.shape)
    outer = (((0,), (0,)), ((), ()))
    local_q = lax.dot_general(flat, dq, outer, preferred_element_type=jnp.float32)
    local_k = lax.dot_general(flat, dk, outer, preferred_element_type=jnp.float32)
    local_v = lax.dot_general(flat, dv, outer, preferred_element_type=jnp.float32)
    sum_q, sum_k, sum_v = lax.psum((local_q, local_k, local_v), ("gx", "gy"))
    mixed = out.reshape(feats.shape)
    return (
        mixed,
        feat_grad,
        sum_q.astype(jnp.bfloat16),
        sum_k.astype(jnp.bfloat16),
        sum_v.astype(jnp.bfloat16),
    )


def solution(mesh):
    return jax.shard_map(
        body,
        mesh=mesh,
        in_specs=(
            P("gx", "gy", None, None, None),
            P(),
            P(),
            P(),
            P("gx", "gy", None, None, None),
            P("gx", "gy"),
            P("gx", "gy", None),
            P("gx", "gy", None, None),
            P("gx", "gy", None, None),
        ),
        out_specs=(P("gx", "gy", None, None, None), P("gx", "gy", None, None, None), P(), P(), P()),
        check_vma=False,
    )
```

profile of v0, /device:TPU:1, one launch (start us, length us, event | category | flops | bytes accessed | tf_op | source)
XLA Modules:
  0.0 444.5 jit_solution(17124175754200817036)
XLA Ops:
  0.7 1.5 convolution_convert_fusion.2
  2.2 1.4 convolution_convert_fusion.3
  3.7 8.8 %collective-permute-start.1 = (bf16[1,1,2,128,1024]{4,3,2,1,0:T(8,128)(2,1)S(1)}, bf16[1,1,2,128,1024]{4,3,2,1,0:T(8,128)(2,1)S(1)}, u32[]{:S(2)}, u32[]{:S(2)}) collective-permute-start(bf16[1,1,2,128,1024]{4,3,2,1,0:T(8,128)(2,1)S(1)} %bitcast.172), channel_id=1, source_target_pairs={{16,0},{32,16},{48,32},{64,48},{80,64},{96,80},{112,96},{128,112},... | collective-permute-start | bytes 1572872 | tf_op jit(solution)/shard_map/ppermute | solution.py:17
  12.5 1.9 collective-permute-start
  15.5 5.0 %collective-permute-done = bf16[1,1,2,128,1024]{4,3,2,1,0:T(8,128)(2,1)S(1)} collective-permute-done((bf16[1,1,2,128,1024]{4,3,2,1,0:T(8,128)(2,1)S(1)}, bf16[1,1,2,128,1024]{4,3,2,1,0:T(8,128)(2,1)S(1)}, u32[]{:S(2)}, u32[]{:S(2)}) %collective-permute-start) | collective-permute-done | bytes 524320 | tf_op jit(solution)/shard_map/ppermute | solution.py:16
  20.5 1.4 pad_maximum_fusion
  21.8 2.5 collective-permute-start.2
  24.4 0.8 copy.22
  25.4 1.3 collective-permute-start.3
  26.6 0.8 constant_dynamic-update-slice_fusion.3
  27.6 1.0 convolution_convert_fusion.1
  28.6 0.8 bitcast_dynamic-update-slice_fusion.1
  29.4 0.9 bitcast_dynamic-update-slice_fusion
  30.3 23.5 %collective-permute-done.2 = bf16[3,1,2,128,1024]{4,3,2,1,0:T(8,128)(2,1)} collective-permute-done((bf16[3,1,2,128,1024]{4,3,2,1,0:T(8,128)(2,1)}, bf16[3,1,2,128,1024]{4,3,2,1,0:T(8,128)(2,1)}, u32[]{:S(2)}, u32[]{:S(2)}) %collective-permute-start.2) | collective-permute-done | bytes 1572896 | tf_op jit(solution)/shard_map/ppermute | solution.py:16
  53.7 1.9 fusion.46
  55.6 38.4 %collective-permute-done.3 = bf16[3,1,2,128,1024]{4,3,2,1,0:T(8,128)(2,1)S(1)} collective-permute-done((bf16[3,1,2,128,1024]{4,3,2,1,0:T(8,128)(2,1)}, bf16[3,1,2,128,1024]{4,3,2,1,0:T(8,128)(2,1)S(1)}, u32[]{:S(2)}, u32[]{:S(2)}) %collective-permute-start.3) | collective-permute-done | bytes 1572896 | tf_op jit(solution)/shard_map/ppermute | solution.py:17
  94.0 0.8 fusion.45
  94.8 3.8 gather_fusion
  98.6 81.0 %while.14 = (s32[]{:T(128)}, bf16[2,128,512]{2,1,0:T(8,128)(2,1)}, bf16[2,128,512]{2,1,0:T(8,128)(2,1)}, f32[2,4,128,1024]{3,2,1,0:T(8,128)}, pred[2,128]{1,0:T(...) while((s32[]{:T(128)}, bf16[2,128,512]{2,1,0:T(8,128)(2,1)}, ...), condition=%wide.region_4.5_spmd, body=%wide.region_0.4_spmd.sunk | while | flops 415043072 | bytes 50373096 | solution.py:66
  99.2 0.9 constant_dynamic-slice_fusion.8
  100.1 0.9 constant_dynamic-slice_fusion.9
  101.1 0.8 copy.62
  101.8 1.3 constant_dynamic-slice_fusion.7
  103.7 0.9 fusion.105
  105.0 3.9 fusion.108
  108.9 2.8 fusion.110
  111.7 8.5 %fusion.109 = bf16[8,64,128]{2,1,0:T(8,128)(2,1)} fusion(bf16[512,8,64]{0,2,1:T(8,128)(2,1)} %bitcast.165, f32[8,128,512]{2,1,0:T(8,128)S(1)} %fusion.107, f32[8,128,512]{2,1,0:T(8,128)} %get-tuple-element.182, f32[8,128]{1,0:T(8,128)S(1)} %copy-done.16), kind=kOutput, calls=%fused_computation.15.clone.1 | convolution fusion | flops 70845952 | bytes 4853760 | tf_op jit(solution)/shard_map/while/body/eval_jaxpr/hqk,khd->qhd/dot_general | solution.py:50
  120.2 8.8 %fusion.111 = f32[512,8,64]{0,2,1:T(8,128)} fusion(bf16[128,8,64]{0,2,1:T(8,128)(2,1)S(1)} %bitcast.180, f32[8,128,512]{2,1,0:T(8,128)S(1)} %fusion.107, f32[8,128,512]{2,1,0:T(8,128)} %get-tuple-element.182, f32[8,128]{1,0:T(8,128)S(1)} %copy-done.16), kind=kOutput, calls=%fused_computation.12.clone.1 | convolution fusion | flops 70780416 | bytes 5378048 | tf_op jit(solution)/shard_map/while/body/eval_jaxpr/hqk,qhd->khd/dot_general | solution.py:52
  129.0 2.0 convolution_bitcast_fusion.5
  131.4 1.6 reshape.187
  132.9 1.8 maximum_bitcast_fusion.2
  134.7 2.0 copy.65
  137.0 0.7 constant_dynamic-update-slice_fusion.6
  137.7 1.5 constant_dynamic-update-slice_fusion.7
  139.7 0.9 constant_dynamic-slice_fusion.8
  140.6 0.9 constant_dynamic-slice_fusion.9
  141.6 0.8 copy.62
  142.3 1.3 constant_dynamic-slice_fusion.7
  144.2 0.9 fusion.105
  145.5 3.9 fusion.108
  149.4 2.8 fusion.110
  152.2 8.5 %fusion.109 = bf16[8,64,128]{2,1,0:T(8,128)(2,1)} fusion(bf16[512,8,64]{0,2,1:T(8,128)(2,1)} %bitcast.165, f32[8,128,512]{2,1,0:T(8,128)S(1)} %fusion.107, f32[8,128,512]{2,1,0:T(8,128)} %get-tuple-element.182, f32[8,128]{1,0:T(8,128)S(1)} %copy-done.16), kind=kOutput, calls=%fused_computation.15.clone.1 | convolution fusion | flops 70845952 | bytes 4853760 | tf_op jit(solution)/shard_map/while/body/eval_jaxpr/hqk,khd->qhd/dot_general | solution.py:50
  160.7 8.8 %fusion.111 = f32[512,8,64]{0,2,1:T(8,128)} fusion(bf16[128,8,64]{0,2,1:T(8,128)(2,1)S(1)} %bitcast.180, f32[8,128,512]{2,1,0:T(8,128)S(1)} %fusion.107, f32[8,128,512]{2,1,0:T(8,128)} %get-tuple-element.182, f32[8,128]{1,0:T(8,128)S(1)} %copy-done.16), kind=kOutput, calls=%fused_computation.12.clone.1 | convolution fusion | flops 70780416 | bytes 5378048 | tf_op jit(solution)/shard_map/while/body/eval_jaxpr/hqk,qhd->khd/dot_general | solution.py:52
  169.6 2.0 convolution_bitcast_fusion.5
  171.9 1.6 reshape.187
  173.5 1.8 maximum_bitcast_fusion.2
  175.3 2.0 copy.65
  177.5 0.7 constant_dynamic-update-slice_fusion.6
  178.2 1.5 constant_dynamic-update-slice_fusion.7
  179.7 4.6 %copy.40 = f32[1,8,128,1024]{3,1,2,0:T(8,128)S(1)} copy(f32[1,8,128,1024]{3,2,1,0:T(8,128)} %bitcast.176) | data formatting | bytes 8388608
  184.3 3.6 convolution_convert_fusion
  187.9 1.9 fusion.50
  190.2 2.1 collective-permute-start.5
  192.3 1.3 collective-permute-start.6
  193.6 4.6 %collective-permute-start.7 = (bf16[2,128,1024]{2,1,0:T(8,128)(2,1)S(1)}, bf16[2,128,1024]{2,1,0:T(8,128)(2,1)S(1)}, u32[]{:S(2)}, u32[]{:S(2)}) collective-permute-start(bf16[2,128,1024]{2,1,0:T(8,128)(2,1)S(1)} %bitcast.193), channel_id=1, source_target_pairs={{0,1},{1,2},{2,3},{3,4},{4,5},{5,6},{6,7},{7,8},{8,9},{9,10},{10,1... | collective-permute-start | bytes 1572872 | tf_op jit(solution)/shard_map/ppermute | solution.py:25
  198.2 2.7 collective-permute-start.4
  201.7 6.4 %collective-permute-done.6 = bf16[2,128,1024]{2,1,0:T(8,128)(2,1)S(1)} collective-permute-done((bf16[2,128,1024]{2,1,0:T(8,128)(2,1)S(1)}, bf16[2,128,1024]{2,1,0:T(8,128)(2,1)S(1)}, u32[]{:S(2)}, u32[]{:S(2)}) %collective-permute-start.6) | collective-permute-done | bytes 524320 | tf_op jit(solution)/shard_map/ppermute | solution.py:25
  208.1 0.9 collective-permute-done.7
  211.0 1.3 convolution_bitcast_fusion.1
  212.3 1.0 fusion.40
  213.4 226.0 %all-reduce.2 = (bf16[512,512]{0,1:T(8,128)(2,1)}, bf16[512,512]{0,1:T(8,128)(2,1)}, bf16[512,512]{0,1:T(8,128)(2,1)S(1)}) all-reduce(f32[512,512]{0,1:T(8,128)S(1)} %convolution_bitcast_fusion.3, f32[512,512]{0,1:T(8,128)S(1)} %convolution_bitcast_fusion.2, ...), channel_id=1, replica_groups=mesh['gx'=32,'gy'=16] {'gx','gy'}, use_global_device_ids=true, to_apply=%region_5.6 | all-reduce | flops 786432 | bytes 4718592 | tf_op jit(solution)/shard_map/psum | solution.py:125
  439.4 2.0 copy.28
  441.4 2.0 copy.29
  443.5 1.0 copy.30
  (95 shorter events, 8.3 us)
Async XLA Ops:
  0.6 26.9 %copy-start = (bf16[512,512]{1,0:T(8,128)(2,1)S(1)}, bf16[512,512]{1,0:T(8,128)(2,1)}, u32[]{:S(2)}) copy-start(bf16[512,512]{1,0:T(8,128)(2,1)} %param.12) | copy-start | bytes 1572868
  0.6 14.4 %copy-start.13 = (s32[1,1,2]{2,1,0:T(1,128)S(1)}, s32[1,1,2]{2,1,0:T(1,128)}, u32[]{:S(2)}) copy-start(s32[1,1,2]{2,1,0:T(1,128)} %param.17) | copy-start | bytes 28
  0.7 14.5 %copy-start.11 = (s32[1,1,2,3]{3,2,1,0:T(2,128)S(1)}, s32[1,1,2,3]{3,2,1,0:T(2,128)}, u32[]{:S(2)}) copy-start(s32[1,1,2,3]{3,2,1,0:T(2,128)} %param.18) | copy-start | bytes 76
  0.7 14.6 %copy-start.12 = (s32[1,1,2,3]{3,2,1,0:T(2,128)S(1)}, s32[1,1,2,3]{3,2,1,0:T(2,128)}, u32[]{:S(2)}) copy-start(s32[1,1,2,3]{3,2,1,0:T(2,128)} %param.19) | copy-start | bytes 76
  3.6 20.9 %copy-start.10 = (bf16[1,1,2,128,512]{4,3,2,1,0:T(8,128)(2,1)S(1)}, bf16[1,1,2,128,512]{4,3,2,1,0:T(8,128)(2,1)}, u32[]{:S(2)}) copy-start(bf16[1,1,2,128,512]{4,3,2,1,0:T(8,128)(2,1)} %param.15) | copy-start | bytes 786436
  3.7 11.8 %collective-permute-start.1 = (bf16[1,1,2,128,1024]{4,3,2,1,0:T(8,128)(2,1)S(1)}, bf16[1,1,2,128,1024]{4,3,2,1,0:T(8,128)(2,1)S(1)}, u32[]{:S(2)}, u32[]{:S(2)}) collective-permute-start(bf16[1,1,2,128,1024]{4,3,2,1,0:T(8,128)(2,1)S(1)} %bitcast.172), channel_id=1, source_target_pairs={{16,0},{32,16},{48,32},{64,48},{80,64},{96,80},{112,96},{128,112},... | collective-permute-start | bytes 1572872 | tf_op jit(solution)/shard_map/ppermute | solution.py:17
  12.5 8.0 %collective-permute-start = (bf16[1,1,2,128,1024]{4,3,2,1,0:T(8,128)(2,1)S(1)}, bf16[1,1,2,128,1024]{4,3,2,1,0:T(8,128)(2,1)S(1)}, u32[]{:S(2)}, u32[]{:S(2)}) collective-permute-start(bf16[1,1,2,128,1024]{4,3,2,1,0:T(8,128)(2,1)S(1)} %bitcast.173), channel_id=1, source_target_pairs={{0,16},{16,32},{32,48},{48,64},{64,80},{80,96},{96,112},{112,128},... | collective-permute-start | bytes 1572872 | tf_op jit(solution)/shard_map/ppermute | solution.py:16
  15.5 12.1 %copy-start.1 = (bf16[1,1,2,128,512]{4,3,2,1,0:T(8,128)(2,1)S(1)}, bf16[1,1,2,128,512]{4,3,2,1,0:T(8,128)(2,1)}, u32[]{:S(2)}) copy-start(bf16[1,1,2,128,512]{4,3,2,1,0:T(8,128)(2,1)} %param.11) | copy-start | bytes 786436
  21.8 31.9 %collective-permute-start.2 = (bf16[3,1,2,128,1024]{4,3,2,1,0:T(8,128)(2,1)}, bf16[3,1,2,128,1024]{4,3,2,1,0:T(8,128)(2,1)}, u32[]{:S(2)}, u32[]{:S(2)}) collective-permute-start(bf16[3,1,2,128,1024]{4,3,2,1,0:T(8,128)(2,1)} %pad_maximum_fusion), channel_id=1, source_target_pairs={{0,1},{1,2},{2,3},{3,4},{4,5},{5,6},{6,7},{7,8},{8,9},{9,10},{10,1... | collective-permute-start | bytes 4718600 | tf_op jit(solution)/shard_map/ppermute | solution.py:16
  25.4 68.6 %collective-permute-start.3 = (bf16[3,1,2,128,1024]{4,3,2,1,0:T(8,128)(2,1)}, bf16[3,1,2,128,1024]{4,3,2,1,0:T(8,128)(2,1)S(1)}, u32[]{:S(2)}, u32[]{:S(2)}) collective-permute-start(bf16[3,1,2,128,1024]{4,3,2,1,0:T(8,128)(2,1)} %pad_maximum_fusion), channel_id=1, source_target_pairs={{1,0},{2,1},{3,2},{4,3},{5,4},{6,5},{7,6},{8,7},{9,8},{10,9},{11,1... | collective-permute-start | bytes 4718600 | tf_op jit(solution)/shard_map/ppermute | solution.py:17
  98.6 0.5 copy-start.14
  108.9 2.8 copy-start.16
  111.7 8.5 %copy-start.3 = (bf16[1,128,512]{1,2,0:T(8,128)(2,1)S(1)}, bf16[1,128,512]{1,2,0:T(8,128)(2,1)}, u32[]{:S(2)}) copy-start(bf16[1,128,512]{1,2,0:T(8,128)(2,1)} %copy.62) | copy-start | bytes 393220 | tf_op jit(solution)/shard_map/while
  134.7 2.0 copy-start.4
  134.7 2.1 copy-start.2
  134.7 2.3 copy-start.7
  137.7 1.5 copy-start.8
  137.7 1.5 copy-start.15
  139.2 0.5 copy-start.14
  149.4 2.8 copy-start.16
  152.2 8.5 %copy-start.3 = (bf16[1,128,512]{1,2,0:T(8,128)(2,1)S(1)}, bf16[1,128,512]{1,2,0:T(8,128)(2,1)}, u32[]{:S(2)}) copy-start(bf16[1,128,512]{1,2,0:T(8,128)(2,1)} %copy.62) | copy-start | bytes 393220 | tf_op jit(solution)/shard_map/while
  175.2 2.0 copy-start.4
  175.3 2.1 copy-start.2
  175.3 2.3 copy-start.7
  178.2 1.5 copy-start.8
  178.2 1.5 copy-start.15
  189.8 11.2 %copy-start.9 = (bf16[2,128,512]{2,1,0:T(8,128)(2,1)S(1)}, bf16[2,128,512]{2,1,0:T(8,128)(2,1)}, u32[]{:S(2)}) copy-start(bf16[2,128,512]{2,1,0:T(8,128)(2,1)} %get-tuple-element.55) | copy-start | bytes 786436
  190.2 11.4 %collective-permute-start.5 = (bf16[2,128,1024]{2,1,0:T(8,128)(2,1)S(1)}, bf16[2,128,1024]{2,1,0:T(8,128)(2,1)S(1)}, u32[]{:S(2)}, u32[]{:S(2)}) collective-permute-start(bf16[2,128,1024]{2,1,0:T(8,128)(2,1)S(1)} %bitcast.195), channel_id=1, source_target_pairs={{0,16},{16,32},{32,48},{48,64},{64,80},{80,96},{96,112},{112,128},... | collective-permute-start | bytes 1572872 | tf_op jit(solution)/shard_map/ppermute | solution.py:25
  192.3 15.8 %collective-permute-start.6 = (bf16[2,128,1024]{2,1,0:T(8,128)(2,1)S(1)}, bf16[2,128,1024]{2,1,0:T(8,128)(2,1)S(1)}, u32[]{:S(2)}, u32[]{:S(2)}) collective-permute-start(bf16[2,128,1024]{2,1,0:T(8,128)(2,1)S(1)} %bitcast.194), channel_id=1, source_target_pairs={{1,0},{2,1},{3,2},{4,3},{5,4},{6,5},{7,6},{8,7},{9,8},{10,9},{11,1... | collective-permute-start | bytes 1572872 | tf_op jit(solution)/shard_map/ppermute | solution.py:25
  193.6 15.3 %collective-permute-start.7 = (bf16[2,128,1024]{2,1,0:T(8,128)(2,1)S(1)}, bf16[2,128,1024]{2,1,0:T(8,128)(2,1)S(1)}, u32[]{:S(2)}, u32[]{:S(2)}) collective-permute-start(bf16[2,128,1024]{2,1,0:T(8,128)(2,1)S(1)} %bitcast.193), channel_id=1, source_target_pairs={{0,1},{1,2},{2,3},{3,4},{4,5},{5,6},{6,7},{7,8},{8,9},{9,10},{10,1... | collective-permute-start | bytes 1572872 | tf_op jit(solution)/shard_map/ppermute | solution.py:25
  198.2 10.7 %collective-permute-start.4 = (bf16[2,128,1024]{2,1,0:T(8,128)(2,1)S(1)}, bf16[2,128,1024]{2,1,0:T(8,128)(2,1)S(1)}, u32[]{:S(2)}, u32[]{:S(2)}) collective-permute-start(bf16[2,128,1024]{2,1,0:T(8,128)(2,1)S(1)} %bitcast.192), channel_id=1, source_target_pairs={{16,0},{32,16},{48,32},{64,48},{80,64},{96,80},{112,96},{128,112},... | collective-permute-start | bytes 1572872 | tf_op jit(solution)/shard_map/ppermute | solution.py:25
  209.6 1.0 copy-start.5
  210.7 1.6 copy-start.6
where the time goes:
time: 446 us; the launch traced here: 444 us
  blocking collectives  226 us (51%)
  waiting for transfers between devices  74.1 us (17%)
  matrix products  64.1 us (14%)
  local copies, waits for them, and re-layouts  45.5 us (10%)
  starting transfers between devices  25.2 us (6%)
  other arithmetic  7.84 us (2%)
    psum x1, blocking collectives, body(): sum_q, sum_k, sum_v = lax.psum((local_q, local_k, local_v), ('gx', 'gy'))  226 us
    ppermute x2, waiting for transfers between devices, with_halo(): after = lax.ppermute(initial, axis, down)  38.4 us
    ppermute x2, waiting for transfers between devices, with_halo(): before = lax.ppermute(last, axis, up)  28.4 us
    dot_general x2, matrix products, one_slot(): jnp.einsum('hqk,qhd->khd', dscore, qh, preferred_element_type=jnp.float32)  17.7 us
    dot_general x2, matrix products, one_slot(): jnp.einsum('hqk,khd->qhd', dscore, kk, preferred_element_type=jnp.float32)  17.1 us
    unnamed x32, local copies, waits for them, and re-layouts  16.2 us
    ppermute x4, starting transfers between devices, passed_along(): lax.ppermute(value, axis, [(source, source + steps) for source in range(i...  10.7 us
    ppermute x2, starting transfers between devices, with_halo(): after = lax.ppermute(initial, axis, down)  10.1 us
  transfers between devices with their start and end apart: 8, of which 5 were waited for; matrix products, arithmetic and copies ran while one was open for 2% of the time, Pallas kernels for 0%

commit v1 on v0

v1 whole, which is shorter than its diff:
```python
import functools

import jax
import jax.numpy as jnp
from jax import lax
from jax.experimental import pallas as pl
from jax.experimental.pallas import tpu as pltpu
from jax.sharding import PartitionSpec as P

HEADS = 8
MESH = pl.DeviceIdType.MESH
VMEM_LIMIT = 56 * 1024 * 1024
F32 = jnp.float32
BF16 = jnp.bfloat16

NT = (((1,), (1,)), ((), ()))
TN = (((0,), (0,)), ((), ()))


def dot(a, b, dims=(((1,), (0,)), ((), ()))):
    return lax.dot_general(a, b, dims, preferred_element_type=F32)


def beside():
    a, b = lax.axis_index("gx"), lax.axis_index("gy")
    na, nb = lax.axis_size("gx"), lax.axis_size("gy")
    return (
        ((a + na - 1) % na, b),
        ((a + 1) % na, b),
        (a, (b + nb - 1) % nb),
        (a, (b + 1) % nb),
    )


def greet(peers):
    barrier = pltpu.get_barrier_semaphore()
    for peer in peers:
        pl.semaphore_signal(barrier, inc=1, device_id=peer, device_id_type=MESH)
    pl.semaphore_wait(barrier, len(peers))


def send(src, dst, send_sem, recv_sem, peer):
    copy = pltpu.make_async_remote_copy(
        src_ref=src,
        dst_ref=dst,
        send_sem=send_sem,
        recv_sem=recv_sem,
        device_id=peer,
        device_id_type=MESH,
    )
    copy.start()
    return copy


def halo_kernel(feats, table, own_sem, send_sem, recv_sem):
    peers = beside()
    own = pltpu.make_async_copy(feats, table.at[pl.ds(0, 2)], own_sem)
    own.start()
    greet(peers)
    copies = []
    for d, peer in enumerate(peers):
        back = d ^ 1
        copies.append(
            send(feats, table.at[pl.ds(2 + 2 * back, 2)], send_sem.at[d], recv_sem.at[back], peer)
        )
    own.wait()
    for copy in copies:
        copy.wait()


def halo(feats):
    slots, points, width = feats.shape
    return pl.pallas_call(
        halo_kernel,
        out_shape=jax.ShapeDtypeStruct((5 * slots, points, width), BF16),
        in_specs=[pl.BlockSpec(memory_space=pltpu.VMEM)],
        out_specs=pl.BlockSpec(memory_space=pltpu.VMEM),
        scratch_shapes=[
            pltpu.SemaphoreType.DMA,
            pltpu.SemaphoreType.DMA((4,)),
            pltpu.SemaphoreType.DMA((4,)),
        ],
        compiler_params=pltpu.CompilerParams(
            collective_id=0, has_side_effects=True, vmem_limit_bytes=VMEM_LIMIT
        ),
        name="halo",
    )(feats)


def attend_kernel(
    patch_count, point_count, neighbours, neighbour_points,
    table, w_query, w_key, w_value, out_grad,
    mixed, own_grad, far_grad, grads,
    rows, keys, values, query, dquery, dkeys, dvalues, total,
):
    slots, points, width = out_grad.shape
    near = neighbours.shape[-1]
    per = (near + 1) * points
    lane = lax.broadcasted_iota(jnp.int32, (points, 128), 1)
    low = lane < 64
    codes = []
    for s in range(slots):
        for m in range(near + 1):
            code = s if m == 0 else neighbours[0, 0, s, m - 1]
            codes.append(code)
            rows[pl.ds((s * (near + 1) + m) * points, points), :] = table[code]
    for s in range(slots):
        query[pl.ds(s * points, points), :] = dot(table[s], w_query[...]).astype(BF16)
    for s in range(slots):
        part = pl.ds(s * per, per)
        keys[part, :] = dot(rows[part, :], w_key[...]).astype(BF16)
        values[part, :] = dot(rows[part, :], w_value[...]).astype(BF16)

    for s in range(slots):
        part = pl.ds(s * per, per)
        count = jnp.where(s < patch_count[0, 0], point_count[0, 0, s], 0)
        live = lax.broadcasted_iota(jnp.int32, (points, 128), 0) < count
        bias = []
        for m in range(near + 1):
            most = point_count[0, 0, s] if m == 0 else neighbour_points[0, 0, s, m - 1]
            dead = lax.broadcasted_iota(jnp.int32, (points, 128), 0) >= most
            bias.append(jnp.where(dead & (lane == 0), -1e30, 0.0).astype(BF16))
        bias = jnp.concatenate(bias, axis=0)
        one = jnp.where(lax.broadcasted_iota(jnp.int32, (2 * points, 128), 1) == 0, 1.0, 0.0).astype(BF16)
        for pair in range(width // 128):
            lanes = pl.ds(pair * 128, 128)
            kk = keys[part, lanes]
            vv = values[part, lanes]
            qq = query[pl.ds(s * points, points), lanes].astype(F32) * 0.125
            gg = jnp.where(live, out_grad[s, :, lanes].astype(F32), 0.0)
            qq = jnp.concatenate([jnp.where(low, qq, 0.0), jnp.where(low, 0.0, qq)], axis=0).astype(BF16)
            gg = jnp.concatenate([jnp.where(low, gg, 0.0), jnp.where(low, 0.0, gg)], axis=0).astype(BF16)
            score = dot(jnp.concatenate([kk, bias], axis=1), jnp.concatenate([qq, one], axis=1), NT)
            dprob = dot(vv, gg, NT)
            top = jnp.max(score, axis=0, keepdims=True)
            expo = jnp.exp(score - top)
            inverse = 1.0 / jnp.sum(expo, axis=0, keepdims=True)
            prob = expo * inverse
            inner = jnp.sum(prob * dprob, axis=0, keepdims=True)
            dscore = (prob * (dprob - inner)).astype(BF16)
            prob = prob.astype(BF16)
            out = dot(vv, prob, TN)
            dq = dot(kk, dscore, TN)
            top_half = lax.broadcasted_iota(jnp.int32, (128, points), 0) < 64
            out = jnp.where(top_half, out[:, :points], out[:, points:]).T
            dq = jnp.where(top_half, dq[:, :points], dq[:, points:]).T
            mixed[s, :, lanes] = jnp.where(live, out, 0.0).astype(BF16)
            dquery[pl.ds(s * points, points), lanes] = (dq * 0.125).astype(BF16)
            dkeys[part, lanes] = dot(dscore, qq).astype(BF16)
            dvalues[part, lanes] = dot(prob, gg).astype(BF16)

    total[...] = jnp.zeros_like(total)
    for s in range(slots):
        part = pl.ds(s * per, per)
        term = dot(dkeys[part, :], w_key[...], NT) + dot(dvalues[part, :], w_value[...], NT)
        total[s] += dot(dquery[pl.ds(s * points, points), :], w_query[...], NT)
        for m in range(near + 1):
            code = codes[s * (near + 1) + m]
            total[code] += term[m * points : (m + 1) * points]
    own_grad[...] = total[pl.ds(0, slots)]
    far_grad[...] = total[pl.ds(slots, 4 * slots)].astype(BF16)
    own = table[pl.ds(0, slots)].reshape(slots * points, width)
    grads[:, :width] = dot(own, dquery[...], TN).astype(BF16)
    grads[:, width : 2 * width] = dot(rows[...], dkeys[...], TN).astype(BF16)
    grads[:, 2 * width :] = dot(rows[...], dvalues[...], TN).astype(BF16)


def attend(patch_count, point_count, neighbours, neighbour_points, table, w_query, w_key, w_value, out_grad):
    slots, points, width = out_grad.shape
    entries = slots * (neighbours.shape[-1] + 1) * points
    smem = pl.BlockSpec(memory_space=pltpu.SMEM)
    vmem = pl.BlockSpec(memory_space=pltpu.VMEM)
    return pl.pallas_call(
        attend_kernel,
        out_shape=[
            jax.ShapeDtypeStruct((slots, points, width), BF16),
            jax.ShapeDtypeStruct((slots, points, width), F32),
            jax.ShapeDtypeStruct((4 * slots, points, width), BF16),
            jax.ShapeDtypeStruct((width, 3 * width), BF16),
        ],
        in_specs=[smem] * 4 + [vmem] * 5,
        out_specs=[vmem] * 4,
        scratch_shapes=[
            pltpu.VMEM((entries, width), BF16),
            pltpu.VMEM((entries, width), BF16),
            pltpu.VMEM((entries, width), BF16),
            pltpu.VMEM((slots * points, width), BF16),
            pltpu.VMEM((slots * points, width), BF16),
            pltpu.VMEM((entries, width), BF16),
            pltpu.VMEM((entries, width), BF16),
            pltpu.VMEM((5 * slots, points, width), F32),
        ],
        compiler_params=pltpu.CompilerParams(vmem_limit_bytes=VMEM_LIMIT),
        name="attend",
    )(patch_count, point_count, neighbours, neighbour_points, table, w_query, w_key, w_value, out_grad)


def reduce_kernel(
    own_grad, far_grad, grads,
    feat_grad, summed,
    back, from_core, half, from1, part1, from2, part2, from3, whole3,
    s_back, r_back, s_core, r_core, s1, r1, s2, r2, s3, r3, s4, r4, s5, r5, s6, r6, s7, r7,
):
    a, b = lax.axis_index("gx"), lax.axis_index("gy")
    core, x, zh = a % 2, (a // 2) % 4, a // 8
    y, zl = b // 4, b % 4
    z = zh * 4 + zl
    wide = grads.shape[1]

    def device(core_=core, x_=x, y_=y, z_=z):
        return ((z_ // 4 * 4 + x_) * 2 + core_, y_ * 4 + z_ % 4)

    sides = beside()
    partner = device(core_=1 - core)
    xs = [(x + k) % 4 for k in range(1, 4)]
    ys = [(y + k) % 4 for k in range(1, 4)]
    zs = [(z + k) % 16 for k in range(1, 16)]
    x_devices = [device(x_=i) for i in xs]
    y_devices = [device(y_=i) for i in ys]
    z_devices = [device(z_=i) for i in zs]
    greet([*sides, partner, *x_devices, *y_devices, *z_devices])

    swap = send(grads.at[pl.ds((1 - core) * 256, 256)], from_core, s_core, r_core, partner)
    returns = [
        send(far_grad.at[pl.ds(2 * d, 2)], back.at[d ^ 1], s_back.at[d], r_back.at[d ^ 1], peer)
        for d, peer in enumerate(sides)
    ]
    swap.wait()
    half[...] = (
        grads[pl.ds(core * 256, 256), :].astype(F32) + from_core[...].astype(F32)
    ).astype(BF16)

    orders = ((x, xs, x_devices, y, ys, y_devices), (y, ys, y_devices, x, xs, x_devices))
    copies = []
    for h, (me, others, devices, _, _, _) in enumerate(orders):
        for k in range(3):
            copies.append(
                send(
                    half.at[pl.ds(h * 128 + others[k] * 32, 32)],
                    from1.at[h, k],
                    s1.at[h, k],
                    r1.at[h, k],
                    devices[k],
                )
            )
    for h, (me, others, devices, _, _, _) in enumerate(orders):
        for k in range(3):
            copies[3 * h + k].wait()
        acc = half[pl.ds(h * 128 + me * 32, 32), :].astype(F32)
        for k in range(3):
            acc = acc + from1[h, k].astype(F32)
        part1[h] = acc.astype(BF16)

    copies = []
    for h, (_, _, _, me, others, devices) in enumerate(orders):
        for k in range(3):
            i = others[k]
            copies.append(
                send(
                    part1.at[h, pl.ds(i // 2 * 16, 16), pl.ds(i % 2 * 768, 768)],
                    from2.at[h, k],
                    s2.at[h, k],
                    r2.at[h, k],
                    devices[k],
                )
            )
    for h, (_, _, _, me, others, devices) in enumerate(orders):
        for k in range(3):
            copies[3 * h + k].wait()
        acc = part1[h, pl.ds(me // 2 * 16, 16), pl.ds(me % 2 * 768, 768)].astype(F32)
        for k in range(3):
            acc = acc + from2[h, k].astype(F32)
        acc = acc.astype(BF16)
        for t in range(6):
            part2[6 * h + t] = acc[:, t * 128 : (t + 1) * 128]
    part2[pl.ds(12, 4)] = jnp.zeros((4, 16, 128), BF16)

    copies = [
        send(part2.at[zs[k]], from3.at[k], s3.at[k], r3.at[k], z_devices[k]) for k in range(15)
    ]
    acc = part2[z].astype(F32)
    for k in range(15):
        copies[k].wait()
        acc = acc + from3[k].astype(F32)
    whole3[z] = acc.astype(BF16)

    copies = [
        send(whole3.at[z], whole3.at[z], s4.at[k], r4.at[k], z_devices[k]) for k in range(15)
    ]
    for copy in copies:
        copy.wait()

    def piece(h, first, second):
        rows = core * 256 + h * 128 + first * 32 + second // 2 * 16
        return summed.at[pl.ds(rows, 16), pl.ds(second % 2 * 768, 768)]

    copies = []
    for h, (first, _, _, second, others, devices) in enumerate(orders):
        mine = piece(h, first, second)
        mine[...] = jnp.concatenate([whole3[6 * h + t] for t in range(6)], axis=1)
        for k in range(3):
            copies.append(send(mine, mine, s5.at[h, k], r5.at[h, k], devices[k]))
    for copy in copies:
        copy.wait()
    copies = []
    for h, (first, others, devices, _, _, _) in enumerate(orders):
        mine = summed.at[pl.ds(core * 256 + h * 128 + first * 32, 32)]
        for k in range(3):
            copies.append(send(mine, mine, s6.at[h, k], r6.at[h, k], devices[k]))
    for copy in copies:
        copy.wait()
    mine = summed.at[pl.ds(core * 256, 256)]
    swap = send(mine, mine, s7, r7, partner)

    for copy in returns:
        copy.wait()
    acc = own_grad[...]
    for d in range(4):
        acc = acc + back[d].astype(F32)
    feat_grad[...] = acc.astype(BF16)
    swap.wait()


def reduce(own_grad, far_grad, grads):
    slots, points, width = own_grad.shape
    dma = pltpu.SemaphoreType.DMA
    vmem = pl.BlockSpec(memory_space=pltpu.VMEM)
    return pl.pallas_call(
        reduce_kernel,
        out_shape=[
            jax.ShapeDtypeStruct((slots, points, width), BF16),
            jax.ShapeDtypeStruct((width, 3 * width), BF16),
        ],
        in_specs=[vmem] * 3,
        out_specs=[vmem] * 2,
        scratch_shapes=[
            pltpu.VMEM((4, slots, points, width), BF16),
            pltpu.VMEM((256, 1536), BF16),
            pltpu.VMEM((256, 1536), BF16),
            pltpu.VMEM((2, 3, 32, 1536), BF16),
            pltpu.VMEM((2, 32, 1536), BF16),
            pltpu.VMEM((2, 3, 16, 768), BF16),
            pltpu.VMEM((16, 16, 128), BF16),
            pltpu.VMEM((15, 16, 128), BF16),
            pltpu.VMEM((16, 16, 128), BF16),
            dma((4,)), dma((4,)),
            dma, dma,
            dma((2, 3)), dma((2, 3)),
            dma((2, 3)), dma((2, 3)),
            dma((15,)), dma((15,)),
            dma((15,)), dma((15,)),
            dma((2, 3)), dma((2, 3)),
            dma((2, 3)), dma((2, 3)),
            dma, dma,
        ],
        compiler_params=pltpu.CompilerParams(
            collective_id=1, has_side_effects=True, vmem_limit_bytes=VMEM_LIMIT
        ),
        name="reduce",
    )(own_grad, far_grad, grads)


def body(
    feats, w_query, w_key, w_value, out_grad, patch_count, point_count, neighbours, neighbour_points
):
    slots, points, width = (feats.shape[2], feats.shape[3], feats.shape[4])
    own = feats.reshape(slots, points, width)
    table = halo(own)
    mixed, own_grad, far_grad, grads = attend(
        patch_count, point_count, neighbours, neighbour_points,
        table, w_query, w_key, w_value, out_grad.reshape(slots, points, width),
    )
    feat_grad, summed = reduce(own_grad, far_grad, grads)
    return (
        mixed.reshape(feats.shape),
        feat_grad.reshape(feats.shape),
        summed[:, :width],
        summed[:, width : 2 * width],
        summed[:, 2 * width :],
    )


def solution(mesh):
    return jax.shard_map(
        body,
        mesh=mesh,
        in_specs=(
            P("gx", "gy", None, None, None),
            P(),
            P(),
            P(),
            P("gx", "gy", None, None, None),
            P("gx", "gy"),
            P("gx", "gy", None),
            P("gx", "gy", None, None),
            P("gx", "gy", None, None),
        ),
        out_specs=(P("gx", "gy", None, None, None), P("gx", "gy", None, None, None), P(), P(), P()),
        check_vma=False,
    )
```

time: 446 us -> 116 us (0.26)
  blocking collectives: 226 us -> 0 us
  Pallas kernels: 0 us -> 111 us
  waiting for transfers between devices: 74.1 us -> 0 us
  matrix products: 64.1 us -> 0 us
  local copies, waits for them, and re-layouts: 45.5 us -> 3.29 us
  starting transfers between devices: 25.2 us -> 0 us
  other arithmetic: 7.84 us -> 0 us
    psum x1 -> x0, blocking collectives: 226 us -> none  [body(): sum_q, sum_k, sum_v = lax.psum((local_q, local_k, local_v), ('gx', 'gy'))]
    pallas_call x0 -> x3, Pallas kernels: none -> 111 us  [the longest x1 78.7 us: reduce(): pl.pallas_call(reduce_kernel, out_shape=[jax.ShapeDtypeStruct((slots, poi...]
    ppermute x8 -> x0, waiting for transfers between devices: 74.1 us -> none  [the longest x2 38.4 us: with_halo(): after = lax.ppermute(initial, axis, down)]
    dot_general x20 -> x0, matrix products: 56.4 us -> none  [the longest x2 17.7 us: one_slot(): jnp.einsum('hqk,qhd->khd', dscore, qh, preferred_element_type=jnp.float32)]
    ppermute x8 -> x0, starting transfers between devices: 25.2 us -> none  [the longest x4 10.7 us: passed_along(): lax.ppermute(value, axis, [(source, source + steps) for source in range(i...]
    unnamed x32 -> x3, local copies, waits for them, and re-layouts: 16.2 us -> 0.71 us
    dynamic_slice x12 -> x0, local copies, waits for them, and re-layouts: 8.91 us -> none  [attend(): lax.map(one_slot, (query, keys, key_valid, q_valid, grad_out))]
    dynamic_update_slice x10 -> x0, local copies, waits for them, and re-layouts: 8.7 us -> none  [attend(): lax.map(one_slot, (query, keys, key_valid, q_valid, grad_out))]
  transfers between devices with their start and end apart: 8 -> 0, of which waited for: 5 -> 0; matrix products, arithmetic and copies ran while one was open for 2% -> 0% of each run, Pallas kernels for 0% -> 0%
where the time goes in v1:
time: 116 us
  Pallas kernels  111 us (96%)
  local copies, waits for them, and re-layouts  3.29 us (3%)
  between operations  1.3 us (1%)
    pallas_call x1, Pallas kernels, reduce(): pl.pallas_call(reduce_kernel, out_shape=[jax.ShapeDtypeStruct((slots, poi...  78.7 us
    pallas_call x1, Pallas kernels, halo(): pl.pallas_call(halo_kernel, out_shape=jax.ShapeDtypeStruct((5 * slots, po...  19.4 us
    pallas_call x1, Pallas kernels, attend(): pl.pallas_call(attend_kernel, out_shape=[jax.ShapeDtypeStruct((slots, poi...  12.8 us
    slice x1, local copies, waits for them, and re-layouts, body(): summed[:, 2 * width:]  2.58 us

profile of v1, /device:TPU:1, one launch (start us, length us, event | category | flops | bytes accessed | tf_op | source)
XLA Modules:
  0.0 115.6 jit_solution(6562587704630991904)
XLA Ops:
  1.3 19.4 %halo.1.table = bf16[10,128,512]{2,1,0:T(8,128)(2,1)} custom-call(bf16[2,128,512]{2,1,0:T(8,128)(2,1)} %bitcast.6), custom_call_target="tpu_custom_call" | custom-call | tf_op jit(solution)/shard_map/halo/pallas_call | solution.py:73
  20.7 12.8 %attend.1 = (bf16[2,128,512]{2,1,0:T(8,128)(2,1)}, f32[2,128,512]{2,1,0:T(8,128)}, bf16[8,128,512]{2,1,0:T(8,128)(2,1)}, bf16[512,1536]{1,0:T(8,128)(2,1)}) custom-call(s32[1,1]{1,0:T(1,128)S(6)} %copy.15.patch_count, s32[1,1,2]{2,1,0:T(1,128)} %point_count.1, s32[1,1,2,3]{3,2,1,0:T(2,128)} %neighbours.1, s32[1,1,2,3]{3,2,1,0:T(2,128)} %neighbour_points.1, ...), custom_call_target="tpu_custom_call" | custom-call | tf_op jit(solution)/shard_map/attend/pallas_call | solution.py:173
  33.5 78.7 %reduce.1 = (bf16[2,128,512]{2,1,0:T(8,128)(2,1)}, bf16[512,1536]{1,0:T(8,128)(2,1)}) custom-call(f32[2,128,512]{2,1,0:T(8,128)} %get-tuple-element.12.own_grad, bf16[8,128,512]{2,1,0:T(8,128)(2,1)} %get-tuple-element.13.far_grad, bf16[512,1536]{1,0:T(8,128)(2,1)} %get-tuple-element.14.grads), custom_call_target="tpu_custom_call" | custom-call | tf_op jit(solution)/shard_map/reduce/pallas_call | solution.py:328
  112.3 0.0 copy-start
  112.3 2.6 %fusion = (bf16[512,512]{1,0:T(8,128)(2,1)}, bf16[512,512]{1,0:T(8,128)(2,1)}, bf16[512,512]{1,0:T(8,128)(2,1)}) fusion(bf16[512,1536]{1,0:T(8,128)(2,1)} %get-tuple-element.16), kind=kLoop, calls=%fused_computation | loop fusion | bytes 3145728 | tf_op jit(solution)/shard_map/slice | solution.py:379
  114.9 0.0 copy-done
  114.9 0.7 copy.16
Async XLA Ops:
  112.3 2.6 %copy-start = (bf16[2,128,512]{2,1,0:T(8,128)(2,1)S(1)}, bf16[2,128,512]{2,1,0:T(8,128)(2,1)}, u32[]{:S(2)}) copy-start(bf16[2,128,512]{2,1,0:T(8,128)(2,1)} %get-tuple-element.15) | copy-start | bytes 786436

commit v2 on v1

--- a/solution.py
+++ b/solution.py
@@ -19,24 +19,6 @@
 
 def dot(a, b, dims=(((1,), (0,)), ((), ()))):
     return lax.dot_general(a, b, dims, preferred_element_type=F32)
-
-
-def beside():
-    a, b = lax.axis_index("gx"), lax.axis_index("gy")
-    na, nb = lax.axis_size("gx"), lax.axis_size("gy")
-    return (
-        ((a + na - 1) % na, b),
-        ((a + 1) % na, b),
-        (a, (b + nb - 1) % nb),
-        (a, (b + 1) % nb),
-    )
-
-
-def greet(peers):
-    barrier = pltpu.get_barrier_semaphore()
-    for peer in peers:
-        pl.semaphore_signal(barrier, inc=1, device_id=peer, device_id_type=MESH)
-    pl.semaphore_wait(barrier, len(peers))
 
 
 def send(src, dst, send_sem, recv_sem, peer):
@@ -52,20 +34,126 @@
     return copy
 
 
-def halo_kernel(feats, table, own_sem, send_sem, recv_sem):
-    peers = beside()
+class Place:
+    def __init__(self):
+        a, b = lax.axis_index("gx"), lax.axis_index("gy")
+        self.core, self.x, self.zh, self.y, self.zl = a % 2, (a // 2) % 4, a // 8, b // 4, b % 4
+        self.other = 1 - self.core
+        self.edge = self.x == 3 * self.core
+        self.partner = self.at(core=self.other)
+        self.outer = ((a + 31 + 2 * self.core) % 32, b)
+        self.down, self.up = (a, (b + 15) % 16), (a, (b + 1) % 16)
+        self.source = self.at(x=3 * self.core)
+        self.final = self.at(core=self.other, x=3 * self.other, zh=(self.zh + 3 + 2 * self.core) % 4)
+        self.reached = [
+            self.at(core=self.other, x=p, zh=(self.zh + 3 + 2 * self.core) % 4) for p in range(4)
+        ]
+        self.turn = [(self.x + k) % 4 for k in range(1, 4)]
+
+    def at(self, core=None, x=None, zh=None, y=None, zl=None):
+        core = self.core if core is None else core
+        x = self.x if x is None else x
+        zh = self.zh if zh is None else zh
+        y = self.y if y is None else y
+        zl = self.zl if zl is None else zl
+        return ((zh * 4 + x) * 2 + core, y * 4 + zl)
+
+
+def signal(peers):
+    barrier = pltpu.get_barrier_semaphore()
+    for peer in peers:
+        pl.semaphore_signal(barrier, inc=1, device_id=peer, device_id_type=MESH)
+
+
+def greet(here, peers):
+    barrier = pltpu.get_barrier_semaphore()
+    peers = [here.partner, here.down, here.up, *peers]
+    signal(peers)
+
+    @pl.when(here.edge)
+    def _():
+        signal([here.at(x=p) for p in here.turn] + here.reached)
+        pl.semaphore_wait(barrier, len(peers) + 7)
+
+    @pl.when(jnp.logical_not(here.edge))
+    def _():
+        signal([here.source, here.final, here.outer])
+        pl.semaphore_wait(barrier, len(peers) + 3)
+
+
+def quarter(ref, p):
+    return ref.at[p // 2, pl.ds(p % 2 * 64, 64)]
+
+
+def flat_wait(ref, sem):
+    pltpu.make_async_copy(ref, ref, sem).wait()
+
+
+EXCHANGE_SCRATCH = [
+    pltpu.VMEM((64, 512), BF16),
+    pltpu.SemaphoreType.DMA((4,)),
+    pltpu.SemaphoreType.DMA((4,)),
+    pltpu.SemaphoreType.DMA((4,)),
+    pltpu.SemaphoreType.DMA((4,)),
+    pltpu.SemaphoreType.DMA((2,)),
+]
+
+
+def exchange_start(here, src, dst, relay, s, r, sq, rq, hop):
+    @pl.when(here.edge)
+    def _():
+        for p in here.turn:
+            send(quarter(src[1], p), relay, sq.at[p], hop.at[0], here.at(x=p))
+        send(quarter(src[1], here.x), quarter(dst[1], here.x), sq.at[here.x], rq.at[here.x], here.final)
+
+    send(src[3], dst[2], s.at[3], r.at[2], here.up)
+    send(src[2], dst[3], s.at[2], r.at[3], here.down)
+    send(src[0], dst[0], s.at[0], r.at[0], here.partner)
+
+    @pl.when(jnp.logical_not(here.edge))
+    def _():
+        send(src[1], dst[1], s.at[1], r.at[1], here.outer)
+
+
+def exchange_relay(here, src, dst, relay, s, r, sq, rq, hop):
+    @pl.when(jnp.logical_not(here.edge))
+    def _():
+        flat_wait(relay, hop.at[0])
+        send(relay, quarter(dst[1], here.x), hop.at[1], rq.at[here.x], here.final)
+
+
+def exchange_finish(here, src, dst, relay, s, r, sq, rq, hop):
+    for d in (0, 2, 3):
+        flat_wait(dst[d], r.at[d])
+
+    @pl.when(here.edge)
+    def _():
+        for p in range(4):
+            flat_wait(relay, rq.at[p])
+        for p in range(4):
+            flat_wait(relay, sq.at[p])
+
+    @pl.when(jnp.logical_not(here.edge))
+    def _():
+        flat_wait(dst[1], r.at[1])
+        flat_wait(src[1], s.at[1])
+        flat_wait(relay, hop.at[1])
+
+    for d in (0, 2, 3):
+        flat_wait(src[d], s.at[d])
+
+
+def halo_kernel(feats, table, own_sem, *scratch):
+    here = Place()
     own = pltpu.make_async_copy(feats, table.at[pl.ds(0, 2)], own_sem)
     own.start()
-    greet(peers)
-    copies = []
-    for d, peer in enumerate(peers):
-        back = d ^ 1
-        copies.append(
-            send(feats, table.at[pl.ds(2 + 2 * back, 2)], send_sem.at[d], recv_sem.at[back], peer)
-        )
+    greet(here, [])
+    src = [feats] * 4
+    dst = [table.at[pl.ds(2 + 2 * d, 2)] for d in range(4)]
+    exchange_start(here, src, dst, *scratch)
+    exchange_relay(here, src, dst, *scratch)
     own.wait()
-    for copy in copies:
-        copy.wait()
+    exchange_finish(here, src, dst, *scratch)
 
 
 def halo(feats):
@@ -75,16 +163,17 @@
         out_shape=jax.ShapeDtypeStruct((5 * slots, points, width), BF16),
         in_specs=[pl.BlockSpec(memory_space=pltpu.VMEM)],
         out_specs=pl.BlockSpec(memory_space=pltpu.VMEM),
-        scratch_shapes=[
-            pltpu.SemaphoreType.DMA,
-            pltpu.SemaphoreType.DMA((4,)),
-            pltpu.SemaphoreType.DMA((4,)),
-        ],
+        scratch_shapes=[pltpu.SemaphoreType.DMA, *EXCHANGE_SCRATCH],
         compiler_params=pltpu.CompilerParams(
             collective_id=0, has_side_effects=True, vmem_limit_bytes=VMEM_LIMIT
         ),
         name="halo",
     )(feats)
+
+
+def side_of(code, even):
+    swapped = jnp.where(code < 4, code + 2, code - 2)
+    return jnp.where(even & (code >= 2) & (code < 6), swapped, code)
 
 
 def attend_kernel(
@@ -98,10 +187,11 @@
     per = (near + 1) * points
     lane = lax.broadcasted_iota(jnp.int32, (points, 128), 1)
     low = lane < 64
+    even = lax.axis_index("gx") % 2 == 0
     codes = []
     for s in range(slots):
         for m in range(near + 1):
-            code = s if m == 0 else neighbours[0, 0, s, m - 1]
+            code = s if m == 0 else side_of(neighbours[0, 0, s, m - 1], even)
             codes.append(code)
             rows[pl.ds((s * (near + 1) + m) * points, points), :] = table[code]
     for s in range(slots):
@@ -195,169 +285,209 @@
     )(patch_count, point_count, neighbours, neighbour_points, table, w_query, w_key, w_value, out_grad)
 
 
+RETURN_AT = 4
+
+
 def reduce_kernel(
-    own_grad, far_grad, grads,
-    feat_grad, summed,
-    back, from_core, half, from1, part1, from2, part2, from3, whole3,
-    s_back, r_back, s_core, r_core, s1, r1, s2, r2, s3, r3, s4, r4, s5, r5, s6, r6, s7, r7,
+    far_grad, grads,
+    back, summed,
+    from0, half, from1, part1, from2, part2, from3, from4, whole,
+    s0, r0, s1, r1, s2, r2, s3, r3, s4, r4, s5, r5, s6, r6, s7, r7, s8, r8,
+    *scratch,
 ):
-    a, b = lax.axis_index("gx"), lax.axis_index("gy")
-    core, x, zh = a % 2, (a // 2) % 4, a // 8
-    y, zl = b // 4, b % 4
-    z = zh * 4 + zl
-    wide = grads.shape[1]
-
-    def device(core_=core, x_=x, y_=y, z_=z):
-        return ((z_ // 4 * 4 + x_) * 2 + core_, y_ * 4 + z_ % 4)
-
-    sides = beside()
-    partner = device(core_=1 - core)
-    xs = [(x + k) % 4 for k in range(1, 4)]
-    ys = [(y + k) % 4 for k in range(1, 4)]
-    zs = [(z + k) % 16 for k in range(1, 16)]
-    x_devices = [device(x_=i) for i in xs]
-    y_devices = [device(y_=i) for i in ys]
-    z_devices = [device(z_=i) for i in zs]
-    greet([*sides, partner, *x_devices, *y_devices, *z_devices])
-
-    swap = send(grads.at[pl.ds((1 - core) * 256, 256)], from_core, s_core, r_core, partner)
-    returns = [
-        send(far_grad.at[pl.ds(2 * d, 2)], back.at[d ^ 1], s_back.at[d], r_back.at[d ^ 1], peer)
-        for d, peer in enumerate(sides)
-    ]
-    swap.wait()
-    half[...] = (
-        grads[pl.ds(core * 256, 256), :].astype(F32) + from_core[...].astype(F32)
-    ).astype(BF16)
+    here = Place()
+    core, x, y, zh, zl = here.core, here.x, here.y, here.zh, here.zl
+    xs, ys, hs, ls = ([(i + k) % 4 for k in range(1, 4)] for i in (x, y, zh, zl))
+    x_devices = [here.at(x=i) for i in xs]
+    y_devices = [here.at(y=i) for i in ys]
+    h_devices = [here.at(zh=i) for i in hs]
+    l_devices = [here.at(zl=i) for i in ls]
+    greet(here, [*x_devices, *y_devices, *h_devices, *l_devices])
+    src = [far_grad.at[pl.ds(2 * d, 2)] for d in range(4)]
+    dst = [back.at[d] for d in range(4)]
+
+    def returns(at):
+        if at == RETURN_AT:
+            exchange_start(here, src, dst, *scratch)
+        if at == RETURN_AT + 1:
+            exchange_relay(here, src, dst, *scratch)
 
     orders = ((x, xs, x_devices, y, ys, y_devices), (y, ys, y_devices, x, xs, x_devices))
-    copies = []
-    for h, (me, others, devices, _, _, _) in enumerate(orders):
-        for k in range(3):
-            copies.append(
-                send(
-                    half.at[pl.ds(h * 128 + others[k] * 32, 32)],
-                    from1.at[h, k],
-                    s1.at[h, k],
-                    r1.at[h, k],
-                    devices[k],
-                )
+    pieces = [(h, k) for k in range(3) for h in range(2)] + [(0, 3), (1, 3)]
+
+    def row_of(h, k):
+        return h * 128 + (orders[h][1][k] if k < 3 else orders[h][0]) * 32
+
+    swaps = []
+    for n, (h, k) in enumerate(pieces):
+        row = row_of(h, k)
+        swaps.append(
+            send(
+                grads.at[pl.ds(here.other * 256 + row, 32)],
+                from0.at[pl.ds(row, 32)],
+                s0.at[n],
+                r0.at[n],
+                here.partner,
             )
-    for h, (me, others, devices, _, _, _) in enumerate(orders):
-        for k in range(3):
-            copies[3 * h + k].wait()
+        )
+    returns(0)
+    first = {}
+    for n, (h, k) in enumerate(pieces):
+        row = row_of(h, k)
+        swaps[n].wait_recv()
+        acc = grads[pl.ds(core * 256 + row, 32), :].astype(F32) + from0[pl.ds(row, 32), :].astype(F32)
+        half[pl.ds(row, 32), :] = acc.astype(BF16)
+        if k < 3:
+            first[h, k] = send(
+                half.at[pl.ds(row, 32)], from1.at[h, k], s1.at[h, k], r1.at[h, k], orders[h][2][k]
+            )
+    returns(1)
+    second = {}
+    for h, (me, _, _, _, others, devices) in enumerate(orders):
         acc = half[pl.ds(h * 128 + me * 32, 32), :].astype(F32)
         for k in range(3):
+            first[h, k].wait_recv()
             acc = acc + from1[h, k].astype(F32)
         part1[h] = acc.astype(BF16)
-
-    copies = []
-    for h, (_, _, _, me, others, devices) in enumerate(orders):
         for k in range(3):
             i = others[k]
-            copies.append(
-                send(
-                    part1.at[h, pl.ds(i // 2 * 16, 16), pl.ds(i % 2 * 768, 768)],
-                    from2.at[h, k],
-                    s2.at[h, k],
-                    r2.at[h, k],
-                    devices[k],
-                )
+            second[h, k] = send(
+                part1.at[h, pl.ds(i // 2 * 16, 16), pl.ds(i % 2 * 768, 768)],
+                from2.at[h, k],
+                s2.at[h, k],
+                r2.at[h, k],
+                devices[k],
             )
-    for h, (_, _, _, me, others, devices) in enumerate(orders):
-        for k in range(3):
-            copies[3 * h + k].wait()
+    part2[pl.ds(12, 4)] = jnp.zeros((4, 16, 128), BF16)
+    returns(2)
+    for h, (_, _, _, me, _, _) in enumerate(orders):
         acc = part1[h, pl.ds(me // 2 * 16, 16), pl.ds(me % 2 * 768, 768)].astype(F32)
         for k in range(3):
+            second[h, k].wait_recv()
             acc = acc + from2[h, k].astype(F32)
         acc = acc.astype(BF16)
         for t in range(6):
             part2[6 * h + t] = acc[:, t * 128 : (t + 1) * 128]
-    part2[pl.ds(12, 4)] = jnp.zeros((4, 16, 128), BF16)
-
-    copies = [
-        send(part2.at[zs[k]], from3.at[k], s3.at[k], r3.at[k], z_devices[k]) for k in range(15)
+
+    third = [
+        send(part2.at[pl.ds(ls[k] * 4, 4)], from3.at[k], s3.at[k], r3.at[k], l_devices[k])
+        for k in range(3)
     ]
-    acc = part2[z].astype(F32)
-    for k in range(15):
-        copies[k].wait()
+    acc = part2[pl.ds(zl * 4, 4)].astype(F32)
+    for k in range(3):
+        third[k].wait_recv()
         acc = acc + from3[k].astype(F32)
-    whole3[z] = acc.astype(BF16)
-
-    copies = [
-        send(whole3.at[z], whole3.at[z], s4.at[k], r4.at[k], z_devices[k]) for k in range(15)
+    from4[zh] = acc.astype(BF16)
+    fourth = [
+        send(from4.at[zh], from4.at[zh], s4.at[k], r4.at[k], h_devices[k]) for k in range(3)
     ]
-    for copy in copies:
+    returns(3)
+    for k in range(3):
+        fourth[k].wait_recv()
+    acc = from4[0].astype(F32)
+    for i in range(1, 4):
+        acc = acc + from4[i].astype(F32)
+    mine = whole.at[pl.ds(zl * 4, 4)]
+    mine[...] = acc.astype(BF16)
+    fifth = [send(mine, mine, s5.at[k], r5.at[k], l_devices[k]) for k in range(3)]
+    returns(4)
+    for k in range(3):
+        fifth[k].wait_recv()
+
+    sixth = {}
+    for h, (me, _, _, place, _, devices) in enumerate(orders):
+        mine = summed.at[
+            pl.ds(core * 256 + h * 128 + me * 32 + place // 2 * 16, 16), pl.ds(place % 2 * 768, 768)
+        ]
+        mine[...] = jnp.concatenate([whole[6 * h + t] for t in range(6)], axis=1)
+        for k in range(3):
+            sixth[h, k] = send(mine, mine, s6.at[h, k], r6.at[h, k], devices[k])
+    returns(5)
+    seventh, eighth = {}, []
+    for h, (me, _, devices, _, _, _) in enumerate(orders):
+        for k in range(3):
+            sixth[h, k].wait_recv()
+        mine = summed.at[pl.ds(core * 256 + h * 128 + me * 32, 32)]
+        for k in range(3):
+            seventh[h, k] = send(mine, mine, s7.at[h, k], r7.at[h, k], devices[k])
+        eighth.append(send(mine, mine, s8.at[h, 3], r8.at[h, 3], here.partner))
+    for k in (0, 2, 1):
+        for h, (me, _, _, _, _, _) in enumerate(orders):
+            seventh[h, k].wait_recv()
+            mine = summed.at[pl.ds(core * 256 + h * 128 + (me + 3 - k) % 4 * 32, 32)]
+            eighth.append(send(mine, mine, s8.at[h, k], r8.at[h, k], here.partner))
+    exchange_finish(here, src, dst, *scratch)
+    for copy in eighth:
         copy.wait()
-
-    def piece(h, first, second):
-        rows = core * 256 + h * 128 + first * 32 + second // 2 * 16
-        return summed.at[pl.ds(rows, 16), pl.ds(second % 2 * 768, 768)]
-
-    copies = []
-    for h, (first, _, _, second, others, devices) in enumerate(orders):
-        mine = piece(h, first, second)
-        mine[...] = jnp.concatenate([whole3[6 * h + t] for t in range(6)], axis=1)
-        for k in range(3):
-            copies.append(send(mine, mine, s5.at[h, k], r5.at[h, k], devices[k]))
-    for copy in copies:
-        copy.wait()
-    copies = []
-    for h, (first, others, devices, _, _, _) in enumerate(orders):
-        mine = summed.at[pl.ds(core * 256 + h * 128 + first * 32, 32)]
-        for k in range(3):
-            copies.append(send(mine, mine, s6.at[h, k], r6.at[h, k], devices[k]))
-    for copy in copies:
-        copy.wait()
-    mine = summed.at[pl.ds(core * 256, 256)]
-    swap = send(mine, mine, s7, r7, partner)
-
-    for copy in returns:
-        copy.wait()
-    acc = own_grad[...]
-    for d in range(4):
-        acc = acc + back[d].astype(F32)
-    feat_grad[...] = acc.astype(BF16)
-    swap.wait()
-
-
-def reduce(own_grad, far_grad, grads):
-    slots, points, width = own_grad.shape
+    for copy in [
+        *swaps, *first.values(), *second.values(), *third, *fourth, *fifth,
+        *sixth.values(), *seventh.values(),
+    ]:
+        copy.wait_send()
+
+
+def reduce(far_grad, grads):
+    slots, points, width = far_grad.shape
     dma = pltpu.SemaphoreType.DMA
     vmem = pl.BlockSpec(memory_space=pltpu.VMEM)
     return pl.pallas_call(
         reduce_kernel,
         out_shape=[
-            jax.ShapeDtypeStruct((slots, points, width), BF16),
+            jax.ShapeDtypeStruct((4, slots // 4, points, width), BF16),
             jax.ShapeDtypeStruct((width, 3 * width), BF16),
         ],
-        in_specs=[vmem] * 3,
+        in_specs=[vmem] * 2,
         out_specs=[vmem] * 2,
         scratch_shapes=[
-            pltpu.VMEM((4, slots, points, width), BF16),
             pltpu.VMEM((256, 1536), BF16),
             pltpu.VMEM((256, 1536), BF16),
             pltpu.VMEM((2, 3, 32, 1536), BF16),
             pltpu.VMEM((2, 32, 1536), BF16),
             pltpu.VMEM((2, 3, 16, 768), BF16),
             pltpu.VMEM((16, 16, 128), BF16),
-            pltpu.VMEM((15, 16, 128), BF16),
+            pltpu.VMEM((3, 4, 16, 128), BF16),
+            pltpu.VMEM((4, 4, 16, 128), BF16),
             pltpu.VMEM((16, 16, 128), BF16),
-            dma((4,)), dma((4,)),
-            dma, dma,
+            dma((8,)), dma((8,)),
             dma((2, 3)), dma((2, 3)),
             dma((2, 3)), dma((2, 3)),
-            dma((15,)), dma((15,)),
-            dma((15,)), dma((15,)),
+            dma((3,)), dma((3,)),
+            dma((3,)), dma((3,)),
+            dma((3,)), dma((3,)),
             dma((2, 3)), dma((2, 3)),
             dma((2, 3)), dma((2, 3)),
-            dma, dma,
+            dma((2, 4)), dma((2, 4)),
+            *EXCHANGE_SCRATCH,
         ],
         compiler_params=pltpu.CompilerParams(
             collective_id=1, has_side_effects=True, vmem_limit_bytes=VMEM_LIMIT
         ),
         name="reduce",
-    )(own_grad, far_grad, grads)
+    )(far_grad, grads)
+
+
+def finish_kernel(own_grad, back, summed, feat_grad, *parts):
+    acc = own_grad[...]
+    for d in range(4):
+        acc = acc + back[d].astype(F32)
+    feat_grad[...] = acc.astype(BF16)
+    width = parts[0].shape[1]
+    for i, part in enumerate(parts):
+        part[...] = summed[:, i * width : (i + 1) * width]
+
+
+def finish(own_grad, back, summed):
+    vmem = pl.BlockSpec(memory_space=pltpu.VMEM)
+    width = summed.shape[0]
+    return pl.pallas_call(
+        finish_kernel,
+        out_shape=[jax.ShapeDtypeStruct(own_grad.shape, BF16)]
+        + [jax.ShapeDtypeStruct((width, width), BF16)] * 3,
+        in_specs=[vmem] * 3,
+        out_specs=[vmem] * 4,
+        compiler_params=pltpu.CompilerParams(vmem_limit_bytes=VMEM_LIMIT),
+        name="finish",
+    )(own_grad, back, summed)
 
 
 def body(
@@ -370,14 +500,9 @@
         patch_count, point_count, neighbours, neighbour_points,
         table, w_query, w_key, w_value, out_grad.reshape(slots, points, width),
     )
-    feat_grad, summed = reduce(own_grad, far_grad, grads)
-    return (
-        mixed.reshape(feats.shape),
-        feat_grad.reshape(feats.shape),
-        summed[:, :width],
-        summed[:, width : 2 * width],
-        summed[:, 2 * width :],
-    )
+    back, summed = reduce(far_grad, grads)
+    feat_grad, *sums = finish(own_grad, back, summed)
+    return (mixed.reshape(feats.shape), feat_grad.reshape(feats.shape), *sums)
 
 
 def solution(mesh):

time: 116 us -> 104 us (0.90)
  Pallas kernels: 111 us -> 103 us
  local copies, waits for them, and re-layouts: 3.29 us -> 0 us
    pallas_call x1 -> x2, Pallas kernels: 78.7 us -> 63.9 us  [the longest x1 60.7 us: reduce(): pl.pallas_call(reduce_kernel, out_shape=[jax.ShapeDtypeStruct((4, slots /...]
    pallas_call x1, Pallas kernels: 19.4 us -> 25.8 us  [halo(): pl.pallas_call(halo_kernel, out_shape=jax.ShapeDtypeStruct((5 * slots, po...]
    slice x1 -> x0, local copies, waits for them, and re-layouts: 2.58 us -> none  [body(): summed[:, 2 * width:]]
where the time goes in v2:
time: 104 us
  Pallas kernels  103 us (99%)
  between operations  1.29 us (1%)
    pallas_call x1, Pallas kernels, reduce(): pl.pallas_call(reduce_kernel, out_shape=[jax.ShapeDtypeStruct((4, slots /...  60.7 us
    pallas_call x1, Pallas kernels, halo(): pl.pallas_call(halo_kernel, out_shape=jax.ShapeDtypeStruct((5 * slots, po...  25.8 us
    pallas_call x1, Pallas kernels, attend(): pl.pallas_call(attend_kernel, out_shape=[jax.ShapeDtypeStruct((slots, poi...  12.9 us
    pallas_call x1, Pallas kernels, finish(): pl.pallas_call(finish_kernel, out_shape=[jax.ShapeDtypeStruct(own_grad.sh...  3.15 us

profile of v2, /device:TPU:1, one launch (start us, length us, event | category | flops | bytes accessed | tf_op | source)
XLA Modules:
  0.0 103.8 jit_solution(10115907169850726665)
XLA Ops:
  1.3 25.8 %halo.1.table = bf16[10,128,512]{2,1,0:T(8,128)(2,1)} custom-call(bf16[2,128,512]{2,1,0:T(8,128)(2,1)} %bitcast.5), custom_call_target="tpu_custom_call" | custom-call | tf_op jit(solution)/shard_map/halo/pallas_call | solution.py:161
  27.1 12.9 %attend.1 = (bf16[2,128,512]{2,1,0:T(8,128)(2,1)}, f32[2,128,512]{2,1,0:T(8,128)}, bf16[8,128,512]{2,1,0:T(8,128)(2,1)}, bf16[512,1536]{1,0:T(8,128)(2,1)}) custom-call(s32[1,1]{1,0:T(1,128)S(6)} %copy.14.patch_count, s32[1,1,2]{2,1,0:T(1,128)} %point_count.1, s32[1,1,2,3]{3,2,1,0:T(2,128)} %neighbours.1, s32[1,1,2,3]{3,2,1,0:T(2,128)} %neighbour_points.1, ...), custom_call_target="tpu_custom_call" | custom-call | tf_op jit(solution)/shard_map/attend/pallas_call | solution.py:263
  39.9 60.7 %reduce.1 = (bf16[4,2,128,512]{3,2,1,0:T(8,128)(2,1)}, bf16[512,1536]{1,0:T(8,128)(2,1)}) custom-call(bf16[8,128,512]{2,1,0:T(8,128)(2,1)} %get-tuple-element.17.far_grad, bf16[512,1536]{1,0:T(8,128)(2,1)} %get-tuple-element.18.grads), custom_call_target="tpu_custom_call" | custom-call | tf_op jit(solution)/shard_map/reduce/pallas_call | solution.py:433
  100.7 3.1 %finish.1 = (bf16[2,128,512]{2,1,0:T(8,128)(2,1)}, bf16[512,512]{1,0:T(8,128)(2,1)}, bf16[512,512]{1,0:T(8,128)(2,1)}, bf16[512,512]{1,0:T(8,128)(2,1)}) custom-call(f32[2,128,512]{2,1,0:T(8,128)} %get-tuple-element.16.own_grad, bf16[4,2,128,512]{3,2,1,0:T(8,128)(2,1)} %get-tuple-element.19.back, bf16[512,1536]{1,0:T(8,128)(2,1)} %get-tuple-element.20.summed), custom_call_target="tpu_custom_call" | custom-call | tf_op jit(solution)/shard_map/finish/pallas_call | solution.py:482

commit v3 on v0

v3 whole, which is shorter than its diff:
```python
import functools

import jax
import jax.numpy as jnp
from jax import lax
from jax.experimental import pallas as pl
from jax.experimental.pallas import tpu as pltpu
from jax.sharding import PartitionSpec as P

HEADS = 8
MESH = pl.DeviceIdType.MESH
VMEM_LIMIT = 56 * 1024 * 1024
F32 = jnp.float32
BF16 = jnp.bfloat16

NT = (((1,), (1,)), ((), ()))
TN = (((0,), (0,)), ((), ()))


def dot(a, b, dims=(((1,), (0,)), ((), ()))):
    return lax.dot_general(a, b, dims, preferred_element_type=F32)


def send(src, dst, send_sem, recv_sem, peer):
    copy = pltpu.make_async_remote_copy(
        src_ref=src,
        dst_ref=dst,
        send_sem=send_sem,
        recv_sem=recv_sem,
        device_id=peer,
        device_id_type=MESH,
    )
    copy.start()
    return copy


class Place:
    def __init__(self):
        a, b = lax.axis_index("gx"), lax.axis_index("gy")
        self.core, self.x, self.zh, self.y, self.zl = a % 2, (a // 2) % 4, a // 8, b // 4, b % 4
        self.other = 1 - self.core
        self.edge = self.x == 3 * self.core
        self.partner = self.at(core=self.other)
        self.outer = ((a + 31 + 2 * self.core) % 32, b)
        self.down, self.up = (a, (b + 15) % 16), (a, (b + 1) % 16)
        self.source = self.at(x=3 * self.core)
        self.final = self.at(core=self.other, x=3 * self.other, zh=(self.zh + 3 + 2 * self.core) % 4)
        self.reached = [
            self.at(core=self.other, x=p, zh=(self.zh + 3 + 2 * self.core) % 4) for p in range(4)
        ]
        self.turn = [(self.x + k) % 4 for k in range(1, 4)]

    def at(self, core=None, x=None, zh=None, y=None, zl=None):
        core = self.core if core is None else core
        x = self.x if x is None else x
        zh = self.zh if zh is None else zh
        y = self.y if y is None else y
        zl = self.zl if zl is None else zl
        return ((zh * 4 + x) * 2 + core, y * 4 + zl)


def signal(peers):
    barrier = pltpu.get_barrier_semaphore()
    for peer in peers:
        pl.semaphore_signal(barrier, inc=1, device_id=peer, device_id_type=MESH)


def greet(here, peers):
    barrier = pltpu.get_barrier_semaphore()
    peers = [here.partner, here.down, here.up, *peers]
    signal(peers)

    @pl.when(here.edge)
    def _():
        signal([here.at(x=p) for p in here.turn] + here.reached)
        pl.semaphore_wait(barrier, len(peers) + 7)

    @pl.when(jnp.logical_not(here.edge))
    def _():
        signal([here.source, here.final, here.outer])
        pl.semaphore_wait(barrier, len(peers) + 3)


def quarter(ref, p):
    return ref.at[p // 2, pl.ds(p % 2 * 64, 64)]


def flat_wait(ref, sem):
    pltpu.make_async_copy(ref, ref, sem).wait()


EXCHANGE_SCRATCH = [
    pltpu.VMEM((64, 512), BF16),
    pltpu.SemaphoreType.DMA((4,)),
    pltpu.SemaphoreType.DMA((4,)),
    pltpu.SemaphoreType.DMA((4,)),
    pltpu.SemaphoreType.DMA((4,)),
    pltpu.SemaphoreType.DMA((2,)),
]


def exchange_start(here, src, dst, relay, s, r, sq, rq, hop):
    @pl.when(here.edge)
    def _():
        for p in here.turn:
            send(quarter(src[1], p), relay, sq.at[p], hop.at[0], here.at(x=p))
        send(quarter(src[1], here.x), quarter(dst[1], here.x), sq.at[here.x], rq.at[here.x], here.final)

    send(src[3], dst[2], s.at[3], r.at[2], here.up)
    send(src[2], dst[3], s.at[2], r.at[3], here.down)
    send(src[0], dst[0], s.at[0], r.at[0], here.partner)

    @pl.when(jnp.logical_not(here.edge))
    def _():
        send(src[1], dst[1], s.at[1], r.at[1], here.outer)


def exchange_relay(here, src, dst, relay, s, r, sq, rq, hop):
    @pl.when(jnp.logical_not(here.edge))
    def _():
        flat_wait(relay, hop.at[0])
        send(relay, quarter(dst[1], here.x), hop.at[1], rq.at[here.x], here.final)


def exchange_finish(here, src, dst, relay, s, r, sq, rq, hop):
    for d in (0, 2, 3):
        flat_wait(dst[d], r.at[d])

    @pl.when(here.edge)
    def _():
        for p in range(4):
            flat_wait(relay, rq.at[p])
        for p in range(4):
            flat_wait(relay, sq.at[p])

    @pl.when(jnp.logical_not(here.edge))
    def _():
        flat_wait(dst[1], r.at[1])
        flat_wait(src[1], s.at[1])
        flat_wait(relay, hop.at[1])

    for d in (0, 2, 3):
        flat_wait(src[d], s.at[d])


def side_of(code, even):
    swapped = jnp.where(code < 4, code + 2, code - 2)
    return jnp.where(even & (code >= 2) & (code < 6), swapped, code)


def layer_kernel(
    patch_count, point_count, neighbours, neighbour_points,
    feats, w_query_hbm, w_key_hbm, w_value_hbm, out_grad_hbm,
    mixed, feat_grad, summed,
    w_query, w_key, w_value, out_grad,
    table, rows, turned, keys, values, query, dquery, dkeys, dvalues,
    term, own_grad, far_grad, back,
    away, own, from0, half, from1, part1, from2, part2, from3, from4, whole,
    loads, s0, r0, s1, r1, s2, r2, s3, r3, s4, r4, s5, r5, s6, r6, s7, r7, s8, r8,
    *scratch,
):
    slots, points, width = feats.shape
    near = neighbours.shape[-1]
    entries = near + 1
    per = entries * points
    here = Place()
    core, x, y, zh, zl = here.core, here.x, here.y, here.zh, here.zl
    xs, ys, hs, ls = ([(i + k) % 4 for k in range(1, 4)] for i in (x, y, zh, zl))
    x_devices = [here.at(x=i) for i in xs]
    y_devices = [here.at(y=i) for i in ys]
    h_devices = [here.at(zh=i) for i in hs]
    l_devices = [here.at(zl=i) for i in ls]
    orders = ((x, xs, x_devices, y, ys, y_devices), (y, ys, y_devices, x, xs, x_devices))
    pieces = [(h, k) for k in range(3) for h in range(2)] + [(0, 3), (1, 3)]
    ahead, behind = scratch[: len(scratch) // 2], scratch[len(scratch) // 2 :]

    started = []
    for n, (src, dst) in enumerate(
        [
            (w_query_hbm, w_query),
            (w_key_hbm, w_key),
            (w_value_hbm, w_value),
            (out_grad_hbm, out_grad),
            (feats, table.at[pl.ds(0, slots)]),
        ]
    ):
        started.append(pltpu.make_async_copy(src, dst, loads.at[n]))
        started[-1].start()
    greet(here, [*x_devices, *y_devices, *h_devices, *l_devices])
    src = [feats] * 4
    dst = [table.at[pl.ds(2 + 2 * d, 2)] for d in range(4)]
    exchange_start(here, src, dst, *ahead)

    for copy in started:
        copy.wait()
    for s in range(slots):
        query[pl.ds(s * points, points), :] = dot(feats[s], w_query[...]).astype(BF16)
    for s in range(slots):
        part = pl.ds(s * per, points)
        rows[part, :] = feats[s]
        keys[part, :] = dot(feats[s], w_key[...]).astype(BF16)
        values[part, :] = dot(feats[s], w_value[...]).astype(BF16)
    exchange_relay(here, src, dst, *ahead)
    exchange_finish(here, src, dst, *ahead)

    even = core == 0
    places = []
    for s in range(slots):
        places.append([s] + [side_of(neighbours[0, 0, s, m], even) for m in range(near)])
        for m in range(1, entries):
            rows[pl.ds((s * entries + m) * points, points), :] = table[places[s][m]]
        part = pl.ds(s * per + points, near * points)
        keys[part, :] = dot(rows[part, :], w_key[...]).astype(BF16)
        values[part, :] = dot(rows[part, :], w_value[...]).astype(BF16)
        part = pl.ds(s * per, per)
        turned[:, part] = rows[part, :].T

    lane = lax.broadcasted_iota(jnp.int32, (points, 128), 1)
    row = lax.broadcasted_iota(jnp.int32, (points, 128), 0)
    low = lane < 64
    lives, biases = [], []
    for s in range(slots):
        count = jnp.where(s < patch_count[0, 0], point_count[0, 0, s], 0)
        lives.append(row < count)
        bias = []
        for m in range(entries):
            most = point_count[0, 0, s] if m == 0 else neighbour_points[0, 0, s, m - 1]
            bias.append(jnp.where((row >= most) & (lane == 0), -1e30, 0.0).astype(BF16))
        biases.append(jnp.concatenate(bias, axis=0))
    one = jnp.where(lax.broadcasted_iota(jnp.int32, (2 * points, 128), 1) == 0, 1.0, 0.0).astype(BF16)
    upper = lax.broadcasted_iota(jnp.int32, (128, points), 0) < 64

    def heads(s, pair):
        part = pl.ds(s * per, per)
        mine = pl.ds(s * points, points)
        lanes = pl.ds(pair * 128, 128)
        live = lives[s]
        kk = keys[part, lanes]
        vv = values[part, lanes]
        qq = query[mine, lanes].astype(F32) * 0.125
        gg = jnp.where(live, out_grad[s, :, lanes].astype(F32), 0.0)
        qq = jnp.concatenate([jnp.where(low, qq, 0.0), jnp.where(low, 0.0, qq)], axis=0).astype(BF16)
        gg = jnp.concatenate([jnp.where(low, gg, 0.0), jnp.where(low, 0.0, gg)], axis=0).astype(BF16)
        score = dot(jnp.concatenate([kk, biases[s]], axis=1), jnp.concatenate([qq, one], axis=1), NT)
        dprob = dot(vv, gg, NT)
        top = jnp.max(score, axis=0, keepdims=True)
        expo = jnp.exp(score - top)
        inverse = 1.0 / jnp.sum(expo, axis=0, keepdims=True)
        prob = expo * inverse
        inner = jnp.sum(prob * dprob, axis=0, keepdims=True)
        dscore = (prob * (dprob - inner)).astype(BF16)
        prob = prob.astype(BF16)
        out = dot(vv, prob, TN)
        dq = dot(kk, dscore, TN)
        out = jnp.where(upper, out[:, :points], out[:, points:]).T
        dq = jnp.where(upper, dq[:, :points], dq[:, points:]).T
        mixed[s, :, lanes] = jnp.where(live, out, 0.0).astype(BF16)
        dquery[mine, lanes] = (dq * 0.125).astype(BF16)
        dkeys[part, lanes] = dot(dscore, qq).astype(BF16)
        dvalues[part, lanes] = dot(prob, gg).astype(BF16)

    def gradients(c, which):
        lanes = pl.ds(c * 256, 256)
        side = pl.ds(pl.multiple_of(which * 256, 256), 256)
        of_query = None
        for s in range(slots):
            part = dot(turned[side, pl.ds(s * per, points)], dquery[pl.ds(s * points, points), lanes])
            of_query = part if of_query is None else of_query + part
        return of_query, dot(turned[side, :], dkeys[:, lanes]), dot(turned[side, :], dvalues[:, lanes])

    def row_of(h, k):
        return h * 128 + (orders[h][1][k] if k < 3 else orders[h][0]) * 32

    def chunk(c):
        for i, part in enumerate(gradients(c, here.other)):
            away[c, :, i * 256 : (i + 1) * 256] = part.astype(BF16)
        swaps = []
        for n, (h, k) in enumerate(pieces):
            at = pl.ds(row_of(h, k), 32)
            swaps.append(
                send(away.at[c, at], from0.at[c, at], s0.at[c, n], r0.at[c, n], here.partner)
            )
        for i, part in enumerate(gradients(c, core)):
            own[c, :, i * 256 : (i + 1) * 256] = part
        yield
        first = {}
        for n, (h, k) in enumerate(pieces):
            at = pl.ds(row_of(h, k), 32)
            swaps[n].wait_recv()
            half[c, at, :] = (own[c, at, :] + from0[c, at, :].astype(F32)).astype(BF16)
            if k < 3:
                first[h, k] = send(
                    half.at[c, at], from1.at[c, h, k], s1.at[c, h, k], r1.at[c, h, k], orders[h][2][k]
                )
        yield
        second = {}
        for h, (me, _, _, _, others, devices) in enumerate(orders):
            acc = half[c, pl.ds(h * 128 + me * 32, 32), :].astype(F32)
            for k in range(3):
                first[h, k].wait_recv()
                acc = acc + from1[c, h, k].astype(F32)
            part1[c, h] = acc.astype(BF16)
            for k in range(3):
                i = others[k]
                second[h, k] = send(
                    part1.at[c, h, pl.ds(i // 2 * 16, 16), pl.ds(i % 2 * 384, 384)],
                    from2.at[c, h, k],
                    s2.at[c, h, k],
                    r2.at[c, h, k],
                    devices[k],
                )
        part2[c, pl.ds(6, 2)] = jnp.zeros((2, 16, 128), BF16)
        yield
        for h, (_, _, _, me, _, _) in enumerate(orders):
            acc = part1[c, h, pl.ds(me // 2 * 16, 16), pl.ds(me % 2 * 384, 384)].astype(F32)
            for k in range(3):
                second[h, k].wait_recv()
                acc = acc + from2[c, h, k].astype(F32)
            acc = acc.astype(BF16)
            for t in range(3):
                part2[c, 3 * h + t] = acc[:, t * 128 : (t + 1) * 128]
        third = [
            send(part2.at[c, pl.ds(ls[k] * 2, 2)], from3.at[c, k], s3.at[c, k], r3.at[c, k], l_devices[k])
            for k in range(3)
        ]
        yield
        acc = part2[c, pl.ds(zl * 2, 2)].astype(F32)
        for k in range(3):
            third[k].wait_recv()
            acc = acc + from3[c, k].astype(F32)
        from4[c, zh] = acc.astype(BF16)
        fourth = [
            send(from4.at[c, zh], from4.at[c, zh], s4.at[c, k], r4.at[c, k], h_devices[k])
            for k in range(3)
        ]
        yield
        for k in range(3):
            fourth[k].wait_recv()
        acc = from4[c, 0].astype(F32)
        for i in range(1, 4):
            acc = acc + from4[c, i].astype(F32)
        mine = whole.at[c, pl.ds(zl * 2, 2)]
        mine[...] = acc.astype(BF16)
        fifth = [send(mine, mine, s5.at[c, k], r5.at[c, k], l_devices[k]) for k in range(3)]
        yield
        for k in range(3):
            fifth[k].wait_recv()
        sixth = {}
        for h, (me, _, _, place, _, devices) in enumerate(orders):
            mine = summed.at[
                c, pl.ds(core * 256 + h * 128 + me * 32 + place // 2 * 16, 16), pl.ds(place % 2 * 384, 384)
            ]
            mine[...] = jnp.concatenate([whole[c, 3 * h + t] for t in range(3)], axis=1)
            for k in range(3):
                sixth[h, k] = send(mine, mine, s6.at[c, h, k], r6.at[c, h, k], devices[k])
        yield
        seventh, eighth = {}, []
        for h, (me, _, devices, _, _, _) in enumerate(orders):
            for k in range(3):
                sixth[h, k].wait_recv()
            mine = summed.at[c, pl.ds(core * 256 + h * 128 + me * 32, 32)]
            for k in range(3):
                seventh[h, k] = send(mine, mine, s7.at[c, h, k], r7.at[c, h, k], devices[k])
            eighth.append(send(mine, mine, s8.at[c, h, 3], r8.at[c, h, 3], here.partner))
        yield
        for k in (0, 2, 1):
            for h, (me, _, _, _, _, _) in enumerate(orders):
                seventh[h, k].wait_recv()
                mine = summed.at[c, pl.ds(core * 256 + h * 128 + (me + 3 - k) % 4 * 32, 32)]
                eighth.append(send(mine, mine, s8.at[c, h, k], r8.at[c, h, k], here.partner))
        yield
        for copy in eighth:
            copy.wait()
        for copy in [
            *swaps, *first.values(), *second.values(), *third, *fourth, *fifth,
            *sixth.values(), *seventh.values(),
        ]:
            copy.wait_send()
        yield

    def terms():
        for s in range(slots):
            part = pl.ds(s * per, per)
            value = dot(dkeys[part, :], w_key[...], NT) + dot(dvalues[part, :], w_value[...], NT)
            term[pl.ds(s * entries, entries)] = value.reshape(entries, points, width)
        for t in range(5 * slots):
            acc = None
            for s in range(slots):
                number, at = 0, 0
                for m in reversed(range(entries)):
                    same = places[s][m] == t
                    number = number + jnp.where(same, 1, 0)
                    at = jnp.where(same, m, at)
                value = term[s * entries + at] * number.astype(F32)
                acc = value if acc is None else acc + value
            if t < slots:
                mine = dquery[pl.ds(t * points, points), :]
                own_grad[t] = acc + dot(mine, w_query[...], NT)
            else:
                far_grad[t - slots] = acc.astype(BF16)

    for pair in range(2):
        for s in range(slots):
            heads(s, pair)
    one_chunk, two_chunk = chunk(0), chunk(1)
    next(one_chunk)
    heads(0, 2)
    next(one_chunk)
    heads(1, 2)
    heads(0, 3)
    next(one_chunk)
    heads(1, 3)
    next(one_chunk)
    next(two_chunk)
    next(two_chunk)
    next(one_chunk)
    terms()
    next(two_chunk)
    next(two_chunk)
    next(one_chunk)
    next(two_chunk)
    next(one_chunk)
    next(two_chunk)
    src = [far_grad.at[pl.ds(2 * d, 2)] for d in range(4)]
    dst = [back.at[d] for d in range(4)]
    exchange_start(here, src, dst, *behind)
    next(one_chunk)
    next(two_chunk)
    exchange_relay(here, src, dst, *behind)
    next(one_chunk)
    next(two_chunk)
    next(two_chunk)
    exchange_finish(here, src, dst, *behind)
    acc = own_grad[...]
    for d in range(4):
        acc = acc + back[d].astype(F32)
    feat_grad[...] = acc.astype(BF16)
    next(one_chunk)
    next(two_chunk)


def layer(patch_count, point_count, neighbours, neighbour_points, feats, w_query, w_key, w_value, out_grad):
    slots, points, width = feats.shape
    entries = slots * (neighbours.shape[-1] + 1)
    own, every = slots * points, entries * points
    dma = pltpu.SemaphoreType.DMA
    smem = pl.BlockSpec(memory_space=pltpu.SMEM)
    vmem = pl.BlockSpec(memory_space=pltpu.VMEM)
    hbm = pl.BlockSpec(memory_space=pl.ANY)

    def held(*shape, kind=BF16):
        return pltpu.VMEM(shape, kind)

    return pl.pallas_call(
        layer_kernel,
        out_shape=[
            jax.ShapeDtypeStruct((slots, points, width), BF16),
            jax.ShapeDtypeStruct((slots, points, width), BF16),
            jax.ShapeDtypeStruct((2, 512, 768), BF16),
        ],
        in_specs=[smem] * 4 + [vmem] + [hbm] * 4,
        out_specs=[vmem] * 3,
        scratch_shapes=[
            held(width, width), held(width, width), held(width, width), held(slots, points, width),
            held(5 * slots, points, width),
            held(every, width),
            held(width, every),
            held(every, width), held(every, width),
            held(own, width), held(own, width),
            held(every, width), held(every, width),
            held(entries, points, width, kind=F32),
            held(slots, points, width, kind=F32),
            held(4 * slots, points, width),
            held(4, slots, points, width),
            held(2, 256, 768), held(2, 256, 768, kind=F32),
            held(2, 256, 768), held(2, 256, 768),
            held(2, 2, 3, 32, 768), held(2, 2, 32, 768),
            held(2, 2, 3, 16, 384), held(2, 8, 16, 128),
            held(2, 3, 2, 16, 128), held(2, 4, 2, 16, 128), held(2, 8, 16, 128),
            dma((5,)),
            dma((2, 8)), dma((2, 8)),
            dma((2, 2, 3)), dma((2, 2, 3)),
            dma((2, 2, 3)), dma((2, 2, 3)),
            dma((2, 3)), dma((2, 3)),
            dma((2, 3)), dma((2, 3)),
            dma((2, 3)), dma((2, 3)),
            dma((2, 2, 3)), dma((2, 2, 3)),
            dma((2, 2, 3)), dma((2, 2, 3)),
            dma((2, 2, 4)), dma((2, 2, 4)),
            *EXCHANGE_SCRATCH,
            *EXCHANGE_SCRATCH,
        ],
        compiler_params=pltpu.CompilerParams(
            collective_id=0, has_side_effects=True, vmem_limit_bytes=VMEM_LIMIT
        ),
        name="layer",
    )(patch_count, point_count, neighbours, neighbour_points, feats, w_query, w_key, w_value, out_grad)


def finish_kernel(mixed, feat_grad, summed, mixed_out, feat_grad_out, of_query, of_key, of_value, sems):
    pairs = [(mixed, mixed_out), (feat_grad, feat_grad_out)]
    for i, out in enumerate((of_query, of_key, of_value)):
        for c in range(2):
            pairs.append((summed.at[c, :, pl.ds(i * 256, 256)], out.at[:, pl.ds(c * 256, 256)]))
    copies = [pltpu.make_async_copy(src, dst, sems.at[n]) for n, (src, dst) in enumerate(pairs)]
    for copy in copies:
        copy.start()
    for copy in copies:
        copy.wait()


def finish(mixed, feat_grad, summed):
    hbm = pl.BlockSpec(memory_space=pl.ANY)
    width = mixed.shape[2]
    return pl.pallas_call(
        finish_kernel,
        out_shape=[jax.ShapeDtypeStruct(mixed.shape, BF16)] * 2
        + [jax.ShapeDtypeStruct((width, width), BF16)] * 3,
        in_specs=[hbm] * 3,
        out_specs=[hbm] * 5,
        scratch_shapes=[pltpu.SemaphoreType.DMA((8,))],
        name="finish",
    )(mixed, feat_grad, summed)


def body(
    feats, w_query, w_key, w_value, out_grad, patch_count, point_count, neighbours, neighbour_points
):
    slots, points, width = (feats.shape[2], feats.shape[3], feats.shape[4])
    mixed, feat_grad, summed = layer(
        patch_count, point_count, neighbours, neighbour_points,
        feats.reshape(slots, points, width), w_query, w_key, w_value,
        out_grad.reshape(slots, points, width),
    )
    mixed, feat_grad, *sums = finish(mixed, feat_grad, summed)
    return (mixed.reshape(feats.shape), feat_grad.reshape(feats.shape), *sums)


def solution(mesh):
    return jax.shard_map(
        body,
        mesh=mesh,
        in_specs=(
            P("gx", "gy", None, None, None),
            P(),
            P(),
            P(),
            P("gx", "gy", None, None, None),
            P("gx", "gy"),
            P("gx", "gy", None),
            P("gx", "gy", None, None),
            P("gx", "gy", None, None),
        ),
        out_specs=(P("gx", "gy", None, None, None), P("gx", "gy", None, None, None), P(), P(), P()),
        check_vma=False,
    )
```

time: 446 us -> 156 us (0.35)
  blocking collectives: 226 us -> 0 us
  Pallas kernels: 0 us -> 155 us
  waiting for transfers between devices: 74.1 us -> 0 us
  matrix products: 64.1 us -> 0 us
  local copies, waits for them, and re-layouts: 45.5 us -> 0 us
  starting transfers between devices: 25.2 us -> 0 us
  other arithmetic: 7.84 us -> 0 us
    psum x1 -> x0, blocking collectives: 226 us -> none  [body(): sum_q, sum_k, sum_v = lax.psum((local_q, local_k, local_v), ('gx', 'gy'))]
    pallas_call x0 -> x2, Pallas kernels: none -> 155 us  [the longest x1 90 us: layer(): pl.pallas_call(layer_kernel, out_shape=[jax.ShapeDtypeStruct((slots, poin...]
    ppermute x8 -> x0, waiting for transfers between devices: 74.1 us -> none  [the longest x2 38.4 us: with_halo(): after = lax.ppermute(initial, axis, down)]
    dot_general x20 -> x0, matrix products: 56.4 us -> none  [the longest x2 17.7 us: one_slot(): jnp.einsum('hqk,qhd->khd', dscore, qh, preferred_element_type=jnp.float32)]
    ppermute x8 -> x0, starting transfers between devices: 25.2 us -> none  [the longest x4 10.7 us: passed_along(): lax.ppermute(value, axis, [(source, source + steps) for source in range(i...]
    unnamed x32 -> x0, local copies, waits for them, and re-layouts: 16.2 us -> none
    dynamic_slice x12 -> x0, local copies, waits for them, and re-layouts: 8.91 us -> none  [attend(): lax.map(one_slot, (query, keys, key_valid, q_valid, grad_out))]
    dynamic_update_slice x10 -> x0, local copies, waits for them, and re-layouts: 8.7 us -> none  [attend(): lax.map(one_slot, (query, keys, key_valid, q_valid, grad_out))]
  transfers between devices with their start and end apart: 8 -> 0, of which waited for: 5 -> 0; matrix products, arithmetic and copies ran while one was open for 2% -> 0% of each run, Pallas kernels for 0% -> 0%
where the time goes in v3:
time: 156 us
  Pallas kernels  155 us (99%)
    pallas_call x1, Pallas kernels, layer(): pl.pallas_call(layer_kernel, out_shape=[jax.ShapeDtypeStruct((slots, poin...  90 us
    pallas_call x1, Pallas kernels, finish(): pl.pallas_call(finish_kernel, out_shape=[jax.ShapeDtypeStruct(mixed.shape...  64.7 us

profile of v3, /device:TPU:1, one launch (start us, length us, event | category | flops | bytes accessed | tf_op | source)
XLA Modules:
  0.0 156.0 jit_solution(15816070353551659306)
XLA Ops:
  1.3 90.0 %layer.1 = (bf16[2,128,512]{2,1,0:T(8,128)(2,1)}, bf16[2,128,512]{2,1,0:T(8,128)(2,1)}, bf16[2,512,768]{2,1,0:T(8,128)(2,1)}) custom-call(s32[1,1]{1,0:T(1,128)S(6)} %copy.14.patch_count, s32[1,1,2]{2,1,0:T(1,128)} %point_count.1, s32[1,1,2,3]{3,2,1,0:T(2,128)} %neighbours.1, s32[1,1,2,3]{3,2,1,0:T(2,128)} %neighbour_points.1, bf16[2,128,512]{2,1,0:T(8,128)(2,1)} %bitcast.4, ...), custom_call_target="tpu_custom_call" | custom-call | tf_op jit(solution)/shard_map/layer/pallas_call | solution.py:454
  91.3 64.7 %finish.1 = (bf16[2,128,512]{2,1,0:T(8,128)(2,1)}, bf16[2,128,512]{2,1,0:T(8,128)(2,1)}, bf16[512,512]{1,0:T(8,128)(2,1)}, bf16[512,512]{1,0:T(8,128)(2,1)}, bf16[512,512]{1,0:T(8,128)(2,1)}) custom-call(bf16[2,128,512]{2,1,0:T(8,128)(2,1)} %get-tuple-element.13.mixed, bf16[2,128,512]{2,1,0:T(8,128)(2,1)} %get-tuple-element.14.feat_grad, ...), custom_call_target="tpu_custom_call" | custom-call | tf_op jit(solution)/shard_map/finish/pallas_call | solution.py:515

commit v4 on v3

--- a/solution.py
+++ b/solution.py
@@ -497,15 +497,26 @@
     )(patch_count, point_count, neighbours, neighbour_points, feats, w_query, w_key, w_value, out_grad)
 
 
-def finish_kernel(mixed, feat_grad, summed, mixed_out, feat_grad_out, of_query, of_key, of_value, sems):
-    pairs = [(mixed, mixed_out), (feat_grad, feat_grad_out)]
-    for i, out in enumerate((of_query, of_key, of_value)):
-        for c in range(2):
-            pairs.append((summed.at[c, :, pl.ds(i * 256, 256)], out.at[:, pl.ds(c * 256, 256)]))
-    copies = [pltpu.make_async_copy(src, dst, sems.at[n]) for n, (src, dst) in enumerate(pairs)]
-    for copy in copies:
-        copy.start()
-    for copy in copies:
+def finish_kernel(mixed, feat_grad, summed, *rest):
+    outs, (rows, sums, arrive, leave) = rest[:5], rest[5:]
+    groups = [[(summed.at[c, :, pl.ds(i * 256, 256)], sums.at[i, :, pl.ds(c * 256, 256)]) for c in range(2)] for i in range(3)]
+    groups += [[(mixed, rows.at[0])], [(feat_grad, rows.at[1])]]
+    held = [sums.at[0], sums.at[1], sums.at[2], rows.at[0], rows.at[1]]
+    outs = [*outs[2:], *outs[:2]]
+    loads, n = [], 0
+    for group in groups:
+        loads.append([])
+        for src, dst in group:
+            loads[-1].append(pltpu.make_async_copy(src, dst, arrive.at[n]))
+            loads[-1][-1].start()
+            n += 1
+    stores = []
+    for i, group in enumerate(loads):
+        for copy in group:
+            copy.wait()
+        stores.append(pltpu.make_async_copy(held[i], outs[i], leave.at[i]))
+        stores[-1].start()
+    for copy in stores:
         copy.wait()
 
 
@@ -518,7 +529,13 @@
         + [jax.ShapeDtypeStruct((width, width), BF16)] * 3,
         in_specs=[hbm] * 3,
         out_specs=[hbm] * 5,
-        scratch_shapes=[pltpu.SemaphoreType.DMA((8,))],
+        scratch_shapes=[
+            pltpu.VMEM((2, *mixed.shape), BF16),
+            pltpu.VMEM((3, width, width), BF16),
+            pltpu.SemaphoreType.DMA((8,)),
+            pltpu.SemaphoreType.DMA((5,)),
+        ],
+        compiler_params=pltpu.CompilerParams(vmem_limit_bytes=VMEM_LIMIT),
         name="finish",
     )(mixed, feat_grad, summed)
 

time: 156 us -> 93.9 us (0.60)
  Pallas kernels: 155 us -> 92.4 us
    pallas_call x1, Pallas kernels: 64.7 us -> 2.45 us  [finish(): pl.pallas_call(finish_kernel, out_shape=[jax.ShapeDtypeStruct(mixed.shape...]
where the time goes in v4:
time: 93.9 us; the launch traced here: 93.7 us
  Pallas kernels  92.4 us (98%)
  between operations  1.29 us (1%)
    pallas_call x1, Pallas kernels, layer(): pl.pallas_call(layer_kernel, out_shape=[jax.ShapeDtypeStruct((slots, poin...  90 us
    pallas_call x1, Pallas kernels, finish(): pl.pallas_call(finish_kernel, out_shape=[jax.ShapeDtypeStruct(mixed.shape...  2.45 us

profile of v4, /device:TPU:1, one launch (start us, length us, event | category | flops | bytes accessed | tf_op | source)
XLA Modules:
  0.0 93.7 jit_solution(8044185947918127251)
XLA Ops:
  1.3 90.0 %layer.1 = (bf16[2,128,512]{2,1,0:T(8,128)(2,1)}, bf16[2,128,512]{2,1,0:T(8,128)(2,1)}, bf16[2,512,768]{2,1,0:T(8,128)(2,1)}) custom-call(s32[1,1]{1,0:T(1,128)S(6)} %copy.14.patch_count, s32[1,1,2]{2,1,0:T(1,128)} %point_count.1, s32[1,1,2,3]{3,2,1,0:T(2,128)} %neighbours.1, s32[1,1,2,3]{3,2,1,0:T(2,128)} %neighbour_points.1, bf16[2,128,512]{2,1,0:T(8,128)(2,1)} %bitcast.4, ...), custom_call_target="tpu_custom_call" | custom-call | tf_op jit(solution)/shard_map/layer/pallas_call | solution.py:454
  91.3 2.5 %finish.1 = (bf16[2,128,512]{2,1,0:T(8,128)(2,1)}, bf16[2,128,512]{2,1,0:T(8,128)(2,1)}, bf16[512,512]{1,0:T(8,128)(2,1)}, bf16[512,512]{1,0:T(8,128)(2,1)}, bf16[512,512]{1,0:T(8,128)(2,1)}) custom-call(bf16[2,128,512]{2,1,0:T(8,128)(2,1)} %get-tuple-element.13.mixed, bf16[2,128,512]{2,1,0:T(8,128)(2,1)} %get-tuple-element.14.feat_grad, ...), custom_call_target="tpu_custom_call" | custom-call | tf_op jit(solution)/shard_map/finish/pallas_call | solution.py:526

commit v5 on v4

--- a/solution.py
+++ b/solution.py
@@ -148,6 +148,9 @@
     return jnp.where(even & (code >= 2) & (code < 6), swapped, code)
 
 
+RETURN_AT = 3
+
+
 def layer_kernel(
     patch_count, point_count, neighbours, neighbour_points,
     feats, w_query_hbm, w_key_hbm, w_value_hbm, out_grad_hbm,
@@ -155,8 +158,8 @@
     w_query, w_key, w_value, out_grad,
     table, rows, turned, keys, values, query, dquery, dkeys, dvalues,
     term, own_grad, far_grad, back,
-    away, own, from0, half, from1, part1, from2, part2, from3, from4, whole,
-    loads, s0, r0, s1, r1, s2, r2, s3, r3, s4, r4, s5, r5, s6, r6, s7, r7, s8, r8,
+    away, own, from0, half, from1, part1, from2, tiles,
+    loads, s0, r0, s1, r1, s2, r2, s3, r3, s4, r4, s5, r5, s6, r6,
     *scratch,
 ):
     slots, points, width = feats.shape
@@ -165,13 +168,17 @@
     per = entries * points
     here = Place()
     core, x, y, zh, zl = here.core, here.x, here.y, here.zh, here.zl
-    xs, ys, hs, ls = ([(i + k) % 4 for k in range(1, 4)] for i in (x, y, zh, zl))
-    x_devices = [here.at(x=i) for i in xs]
-    y_devices = [here.at(y=i) for i in ys]
-    h_devices = [here.at(zh=i) for i in hs]
-    l_devices = [here.at(zl=i) for i in ls]
-    orders = ((x, xs, x_devices, y, ys, y_devices), (y, ys, y_devices, x, xs, x_devices))
-    pieces = [(h, k) for k in range(3) for h in range(2)] + [(0, 3), (1, 3)]
+    axes = (("zl", "x", "y"), ("x", "y", "zl"), ("y", "x", "zl"))
+    place = {"x": x, "y": y, "zl": zl, "zh": zh}
+
+    def moved(**steps):
+        return here.at(**{axis: (place[axis] + by) % 4 for axis, by in steps.items()})
+
+    lines = [[moved(**{line: k}) for k in range(1, 4)] for line, _, _ in axes]
+    steps = sorted(((i, j) for i in range(4) for j in range(4) if i + j), key=lambda t: -min(t[0], 4 - t[0]) - t[1])
+    planes = [[moved(**{u: i, v: j}) for i, j in steps] for _, u, v in axes]
+    deep = [moved(zh=k) for k in range(1, 4)]
+    pieces = [(p, k) for k in range(4) for p in range(3)]
     ahead, behind = scratch[: len(scratch) // 2], scratch[len(scratch) // 2 :]
 
     started = []
@@ -186,7 +193,11 @@
     ):
         started.append(pltpu.make_async_copy(src, dst, loads.at[n]))
         started[-1].start()
-    greet(here, [*x_devices, *y_devices, *h_devices, *l_devices])
+    crosswise = [
+        moved(**{u: i, v: j}) for u, v in (("x", "y"), ("x", "zl"), ("y", "zl"))
+        for i in range(1, 4) for j in range(1, 4)
+    ]
+    greet(here, [*lines[0], *lines[1], *lines[2], *deep, *crosswise])
     src = [feats] * 4
     dst = [table.at[pl.ds(2 + 2 * d, 2)] for d in range(4)]
     exchange_start(here, src, dst, *ahead)
@@ -259,122 +270,94 @@
         dkeys[part, lanes] = dot(dscore, qq).astype(BF16)
         dvalues[part, lanes] = dot(prob, gg).astype(BF16)
 
-    def gradients(c, which):
-        lanes = pl.ds(c * 256, 256)
+    def gradients(which):
         side = pl.ds(pl.multiple_of(which * 256, 256), 256)
         of_query = None
         for s in range(slots):
-            part = dot(turned[side, pl.ds(s * per, points)], dquery[pl.ds(s * points, points), lanes])
+            part = dot(turned[side, pl.ds(s * per, points)], dquery[pl.ds(s * points, points), :])
             of_query = part if of_query is None else of_query + part
-        return of_query, dot(turned[side, :], dkeys[:, lanes]), dot(turned[side, :], dvalues[:, lanes])
-
-    def row_of(h, k):
-        return h * 128 + (orders[h][1][k] if k < 3 else orders[h][0]) * 32
-
-    def chunk(c):
-        for i, part in enumerate(gradients(c, here.other)):
-            away[c, :, i * 256 : (i + 1) * 256] = part.astype(BF16)
-        swaps = []
-        for n, (h, k) in enumerate(pieces):
-            at = pl.ds(row_of(h, k), 32)
-            swaps.append(
-                send(away.at[c, at], from0.at[c, at], s0.at[c, n], r0.at[c, n], here.partner)
-            )
-        for i, part in enumerate(gradients(c, core)):
-            own[c, :, i * 256 : (i + 1) * 256] = part
-        yield
-        first = {}
-        for n, (h, k) in enumerate(pieces):
-            at = pl.ds(row_of(h, k), 32)
-            swaps[n].wait_recv()
-            half[c, at, :] = (own[c, at, :] + from0[c, at, :].astype(F32)).astype(BF16)
+        return dot(turned[side, :], dvalues[...]), of_query, dot(turned[side, :], dkeys[...])
+
+    def sums():
+        for p, part in enumerate(gradients(here.other)):
+            away[p] = part.astype(BF16)
+        first = [place[line] for line, _, _ in axes]
+        row_of = [[pl.multiple_of((first[p] + k) % 4 * 64, 64) for k in (1, 2, 3, 0)] for p in range(3)]
+        swaps = {}
+        for p, k in pieces:
+            at = pl.ds(row_of[p][k], 64)
+            swaps[p, k] = send(away.at[p, at], from0.at[p, at], s0.at[p, k], r0.at[p, k], here.partner)
+        for p, part in enumerate(gradients(core)):
+            own[p] = part
+        one = {}
+        for p, k in pieces:
+            at = pl.ds(row_of[p][k], 64)
+            swaps[p, k].wait_recv()
+            acc = own[p, at, :] + from0[p, at, :].astype(F32)
             if k < 3:
-                first[h, k] = send(
-                    half.at[c, at], from1.at[c, h, k], s1.at[c, h, k], r1.at[c, h, k], orders[h][2][k]
-                )
-        yield
-        second = {}
-        for h, (me, _, _, _, others, devices) in enumerate(orders):
-            acc = half[c, pl.ds(h * 128 + me * 32, 32), :].astype(F32)
+                half[p, at, :] = acc.astype(BF16)
+                one[p, k] = send(half.at[p, at], from1.at[p, k], s1.at[p, k], r1.at[p, k], lines[p][k])
+            else:
+                own[p, at, :] = acc
+        yield
+        order = (1, 2, 0)
+        for p in order:
+            acc = own[p, pl.ds(row_of[p][3], 64), :]
             for k in range(3):
-                first[h, k].wait_recv()
-                acc = acc + from1[c, h, k].astype(F32)
-            part1[c, h] = acc.astype(BF16)
+                one[p, k].wait_recv()
+                acc = acc + from1[p, k].astype(F32)
+            for j in range(4):
+                part1[p, j] = acc[:, j * 128 : (j + 1) * 128].astype(BF16)
+            _, u, v = axes[p]
+            for n, (i, j) in enumerate(steps):
+                a, b = (place[u] + i) % 4, (place[v] + j) % 4
+                send(part1.at[p, b, pl.ds(a * 16, 16)], from2.at[p, n], s2.at[p], r2.at[p], planes[p][n])
+        yield
+        for p in order:
+            flat_wait(from2.at[p], r2.at[p])
+            _, u, v = axes[p]
+            acc = part1[p, place[v], pl.ds(place[u] * 16, 16), :].astype(F32)
+            for n in range(15):
+                acc = acc + from2[p, n].astype(F32)
+            tiles[zh, p] = acc.astype(BF16)
+        three = [send(tiles.at[zh], tiles.at[zh], s3.at[k], r3.at[k], deep[k]) for k in range(3)]
+        yield
+        for copy in three:
+            copy.wait_recv()
+        for p in order:
+            acc = tiles[0, p].astype(F32)
+            for i in range(1, 4):
+                acc = acc + tiles[i, p].astype(F32)
+            _, u, v = axes[p]
+            mine = summed.at[
+                p,
+                pl.ds(core * 256 + first[p] * 64 + place[u] * 16, 16),
+                pl.ds(pl.multiple_of(place[v] * 128, 128), 128),
+            ]
+            mine[...] = acc.astype(BF16)
+            for n in range(15):
+                send(mine, mine, s4.at[p], r4.at[p], planes[p][n])
+        yield
+        five, six = {}, []
+        for p in order:
+            flat_wait(from2.at[p], r4.at[p])
+            mine = summed.at[p, pl.ds(core * 256 + first[p] * 64, 64)]
             for k in range(3):
-                i = others[k]
-                second[h, k] = send(
-                    part1.at[c, h, pl.ds(i // 2 * 16, 16), pl.ds(i % 2 * 384, 384)],
-                    from2.at[c, h, k],
-                    s2.at[c, h, k],
-                    r2.at[c, h, k],
-                    devices[k],
-                )
-        part2[c, pl.ds(6, 2)] = jnp.zeros((2, 16, 128), BF16)
-        yield
-        for h, (_, _, _, me, _, _) in enumerate(orders):
-            acc = part1[c, h, pl.ds(me // 2 * 16, 16), pl.ds(me % 2 * 384, 384)].astype(F32)
-            for k in range(3):
-                second[h, k].wait_recv()
-                acc = acc + from2[c, h, k].astype(F32)
-            acc = acc.astype(BF16)
-            for t in range(3):
-                part2[c, 3 * h + t] = acc[:, t * 128 : (t + 1) * 128]
-        third = [
-            send(part2.at[c, pl.ds(ls[k] * 2, 2)], from3.at[c, k], s3.at[c, k], r3.at[c, k], l_devices[k])
-            for k in range(3)
-        ]
-        yield
-        acc = part2[c, pl.ds(zl * 2, 2)].astype(F32)
-        for k in range(3):
-            third[k].wait_recv()
-            acc = acc + from3[c, k].astype(F32)
-        from4[c, zh] = acc.astype(BF16)
-        fourth = [
-            send(from4.at[c, zh], from4.at[c, zh], s4.at[c, k], r4.at[c, k], h_devices[k])
-            for k in range(3)
-        ]
-        yield
-        for k in range(3):
-            fourth[k].wait_recv()
-        acc = from4[c, 0].astype(F32)
-        for i in range(1, 4):
-            acc = acc + from4[c, i].astype(F32)
-        mine = whole.at[c, pl.ds(zl * 2, 2)]
-        mine[...] = acc.astype(BF16)
-        fifth = [send(mine, mine, s5.at[c, k], r5.at[c, k], l_devices[k]) for k in range(3)]
-        yield
-        for k in range(3):
-            fifth[k].wait_recv()
-        sixth = {}
-        for h, (me, _, _, place, _, devices) in enumerate(orders):
-            mine = summed.at[
-                c, pl.ds(core * 256 + h * 128 + me * 32 + place // 2 * 16, 16), pl.ds(place % 2 * 384, 384)
-            ]
-            mine[...] = jnp.concatenate([whole[c, 3 * h + t] for t in range(3)], axis=1)
-            for k in range(3):
-                sixth[h, k] = send(mine, mine, s6.at[c, h, k], r6.at[c, h, k], devices[k])
-        yield
-        seventh, eighth = {}, []
-        for h, (me, _, devices, _, _, _) in enumerate(orders):
-            for k in range(3):
-                sixth[h, k].wait_recv()
-            mine = summed.at[c, pl.ds(core * 256 + h * 128 + me * 32, 32)]
-            for k in range(3):
-                seventh[h, k] = send(mine, mine, s7.at[c, h, k], r7.at[c, h, k], devices[k])
-            eighth.append(send(mine, mine, s8.at[c, h, 3], r8.at[c, h, 3], here.partner))
+                five[p, k] = send(mine, mine, s5.at[p, k], r5.at[p, k], lines[p][k])
+            six.append(send(mine, mine, s6.at[p, 3], r6.at[p, 3], here.partner))
         yield
         for k in (0, 2, 1):
-            for h, (me, _, _, _, _, _) in enumerate(orders):
-                seventh[h, k].wait_recv()
-                mine = summed.at[c, pl.ds(core * 256 + h * 128 + (me + 3 - k) % 4 * 32, 32)]
-                eighth.append(send(mine, mine, s8.at[c, h, k], r8.at[c, h, k], here.partner))
-        yield
-        for copy in eighth:
+            for p in order:
+                five[p, k].wait_recv()
+                mine = summed.at[p, pl.ds(core * 256 + (first[p] + 3 - k) % 4 * 64, 64)]
+                six.append(send(mine, mine, s6.at[p, k], r6.at[p, k], here.partner))
+        yield
+        for copy in six:
             copy.wait()
-        for copy in [
-            *swaps, *first.values(), *second.values(), *third, *fourth, *fifth,
-            *sixth.values(), *seventh.values(),
-        ]:
+        for p in range(3):
+            flat_wait(from2.at[p], s2.at[p])
+            flat_wait(from2.at[p], s4.at[p])
+        for copy in [*swaps.values(), *one.values(), *three, *five.values()]:
             copy.wait_send()
         yield
 
@@ -399,44 +382,26 @@
             else:
                 far_grad[t - slots] = acc.astype(BF16)
 
-    for pair in range(2):
+    for pair in range(4):
         for s in range(slots):
             heads(s, pair)
-    one_chunk, two_chunk = chunk(0), chunk(1)
-    next(one_chunk)
-    heads(0, 2)
-    next(one_chunk)
-    heads(1, 2)
-    heads(0, 3)
-    next(one_chunk)
-    heads(1, 3)
-    next(one_chunk)
-    next(two_chunk)
-    next(two_chunk)
-    next(one_chunk)
-    terms()
-    next(two_chunk)
-    next(two_chunk)
-    next(one_chunk)
-    next(two_chunk)
-    next(one_chunk)
-    next(two_chunk)
     src = [far_grad.at[pl.ds(2 * d, 2)] for d in range(4)]
     dst = [back.at[d] for d in range(4)]
-    exchange_start(here, src, dst, *behind)
-    next(one_chunk)
-    next(two_chunk)
-    exchange_relay(here, src, dst, *behind)
-    next(one_chunk)
-    next(two_chunk)
-    next(two_chunk)
+    chain = sums()
+    next(chain)
+    terms()
+    for at in range(2, 7):
+        next(chain)
+        if at == RETURN_AT:
+            exchange_start(here, src, dst, *behind)
+        if at == RETURN_AT + 1:
+            exchange_relay(here, src, dst, *behind)
     exchange_finish(here, src, dst, *behind)
     acc = own_grad[...]
     for d in range(4):
         acc = acc + back[d].astype(F32)
     feat_grad[...] = acc.astype(BF16)
-    next(one_chunk)
-    next(two_chunk)
+    next(chain)
 
 
 def layer(patch_count, point_count, neighbours, neighbour_points, feats, w_query, w_key, w_value, out_grad):
@@ -456,7 +421,7 @@
         out_shape=[
             jax.ShapeDtypeStruct((slots, points, width), BF16),
             jax.ShapeDtypeStruct((slots, points, width), BF16),
-            jax.ShapeDtypeStruct((2, 512, 768), BF16),
+            jax.ShapeDtypeStruct((3, 512, 512), BF16),
         ],
         in_specs=[smem] * 4 + [vmem] + [hbm] * 4,
         out_specs=[vmem] * 3,
@@ -472,21 +437,18 @@
             held(slots, points, width, kind=F32),
             held(4 * slots, points, width),
             held(4, slots, points, width),
-            held(2, 256, 768), held(2, 256, 768, kind=F32),
-            held(2, 256, 768), held(2, 256, 768),
-            held(2, 2, 3, 32, 768), held(2, 2, 32, 768),
-            held(2, 2, 3, 16, 384), held(2, 8, 16, 128),
-            held(2, 3, 2, 16, 128), held(2, 4, 2, 16, 128), held(2, 8, 16, 128),
+            held(3, 256, 512), held(3, 256, 512, kind=F32),
+            held(3, 256, 512), held(3, 256, 512),
+            held(3, 3, 64, 512), held(3, 4, 64, 128),
+            held(3, 15, 16, 128), held(4, 3, 16, 128),
             dma((5,)),
-            dma((2, 8)), dma((2, 8)),
-            dma((2, 2, 3)), dma((2, 2, 3)),
-            dma((2, 2, 3)), dma((2, 2, 3)),
-            dma((2, 3)), dma((2, 3)),
-            dma((2, 3)), dma((2, 3)),
-            dma((2, 3)), dma((2, 3)),
-            dma((2, 2, 3)), dma((2, 2, 3)),
-            dma((2, 2, 3)), dma((2, 2, 3)),
-            dma((2, 2, 4)), dma((2, 2, 4)),
+            dma((3, 4)), dma((3, 4)),
+            dma((3, 3)), dma((3, 3)),
+            dma((3,)), dma((3,)),
+            dma((3,)), dma((3,)),
+            dma((3,)), dma((3,)),
+            dma((3, 3)), dma((3, 3)),
+            dma((3, 4)), dma((3, 4)),
             *EXCHANGE_SCRATCH,
             *EXCHANGE_SCRATCH,
         ],
@@ -499,7 +461,7 @@
 
 def finish_kernel(mixed, feat_grad, summed, *rest):
     outs, (rows, sums, arrive, leave) = rest[:5], rest[5:]
-    groups = [[(summed.at[c, :, pl.ds(i * 256, 256)], sums.at[i, :, pl.ds(c * 256, 256)]) for c in range(2)] for i in range(3)]
+    groups = [[(summed.at[(i + 1) % 3], sums.at[i])] for i in range(3)]
     groups += [[(mixed, rows.at[0])], [(feat_grad, rows.at[1])]]
     held = [sums.at[0], sums.at[1], sums.at[2], rows.at[0], rows.at[1]]
     outs = [*outs[2:], *outs[:2]]
@@ -532,7 +494,7 @@
         scratch_shapes=[
             pltpu.VMEM((2, *mixed.shape), BF16),
             pltpu.VMEM((3, width, width), BF16),
-            pltpu.SemaphoreType.DMA((8,)),
+            pltpu.SemaphoreType.DMA((5,)),
             pltpu.SemaphoreType.DMA((5,)),
         ],
         compiler_params=pltpu.CompilerParams(vmem_limit_bytes=VMEM_LIMIT),

time: 93.9 us -> 90.3 us (0.962)
  Pallas kernels: 92.4 us -> 88.8 us
    pallas_call x1, Pallas kernels: 90 us -> 86.4 us  [layer(): pl.pallas_call(layer_kernel, out_shape=[jax.ShapeDtypeStruct((slots, poin...]
where the time goes in v5:
time: 90.3 us; the launch traced here: 90.1 us
  Pallas kernels  88.8 us (98%)
  between operations  1.29 us (1%)
    pallas_call x1, Pallas kernels, layer(): pl.pallas_call(layer_kernel, out_shape=[jax.ShapeDtypeStruct((slots, poin...  86.4 us
    pallas_call x1, Pallas kernels, finish(): pl.pallas_call(finish_kernel, out_shape=[jax.ShapeDtypeStruct(mixed.shape...  2.44 us

profile of v5, /device:TPU:1, one launch (start us, length us, event | category | flops | bytes accessed | tf_op | source)
XLA Modules:
  0.0 90.1 jit_solution(8096844095531781657)
XLA Ops:
  1.3 86.4 %layer.1 = (bf16[2,128,512]{2,1,0:T(8,128)(2,1)}, bf16[2,128,512]{2,1,0:T(8,128)(2,1)}, bf16[3,512,512]{2,1,0:T(8,128)(2,1)}) custom-call(s32[1,1]{1,0:T(1,128)S(6)} %copy.14.patch_count, s32[1,1,2]{2,1,0:T(1,128)} %point_count.1, s32[1,1,2,3]{3,2,1,0:T(2,128)} %neighbours.1, s32[1,1,2,3]{3,2,1,0:T(2,128)} %neighbour_points.1, bf16[2,128,512]{2,1,0:T(8,128)(2,1)} %bitcast.4, ...), custom_call_target="tpu_custom_call" | custom-call | tf_op jit(solution)/shard_map/layer/pallas_call | solution.py:419
  87.7 2.4 %finish.1 = (bf16[2,128,512]{2,1,0:T(8,128)(2,1)}, bf16[2,128,512]{2,1,0:T(8,128)(2,1)}, bf16[512,512]{1,0:T(8,128)(2,1)}, bf16[512,512]{1,0:T(8,128)(2,1)}, bf16[512,512]{1,0:T(8,128)(2,1)}) custom-call(bf16[2,128,512]{2,1,0:T(8,128)(2,1)} %get-tuple-element.13.mixed, bf16[2,128,512]{2,1,0:T(8,128)(2,1)} %get-tuple-element.14.feat_grad, ...), custom_call_target="tpu_custom_call" | custom-call | tf_op jit(solution)/shard_map/finish/pallas_call | solution.py:488

commit v6 on v5

--- a/solution.py
+++ b/solution.py
@@ -82,6 +82,8 @@
 
 
 def quarter(ref, p):
+    if len(ref.shape) == 2:
+        return ref.at[pl.ds(p * 32, 32)]
     return ref.at[p // 2, pl.ds(p % 2 * 64, 64)]
 
 
@@ -89,14 +91,15 @@
     pltpu.make_async_copy(ref, ref, sem).wait()
 
 
-EXCHANGE_SCRATCH = [
-    pltpu.VMEM((64, 512), BF16),
-    pltpu.SemaphoreType.DMA((4,)),
-    pltpu.SemaphoreType.DMA((4,)),
-    pltpu.SemaphoreType.DMA((4,)),
-    pltpu.SemaphoreType.DMA((4,)),
-    pltpu.SemaphoreType.DMA((2,)),
-]
+def exchange_scratch(rows):
+    return [
+        pltpu.VMEM((rows, 512), BF16),
+        pltpu.SemaphoreType.DMA((4,)),
+        pltpu.SemaphoreType.DMA((4,)),
+        pltpu.SemaphoreType.DMA((4,)),
+        pltpu.SemaphoreType.DMA((4,)),
+        pltpu.SemaphoreType.DMA((2,)),
+    ]
 
 
 def exchange_start(here, src, dst, relay, s, r, sq, rq, hop):
@@ -148,7 +151,7 @@
     return jnp.where(even & (code >= 2) & (code < 6), swapped, code)
 
 
-RETURN_AT = 3
+RETURN_AT = (2, 3)
 
 
 def layer_kernel(
@@ -179,7 +182,7 @@
     planes = [[moved(**{u: i, v: j}) for i, j in steps] for _, u, v in axes]
     deep = [moved(zh=k) for k in range(1, 4)]
     pieces = [(p, k) for k in range(4) for p in range(3)]
-    ahead, behind = scratch[: len(scratch) // 2], scratch[len(scratch) // 2 :]
+    ahead, *behind = (scratch[i : i + 6] for i in (0, 6, 12))
 
     started = []
     for n, (src, dst) in enumerate(
@@ -385,18 +388,22 @@
     for pair in range(4):
         for s in range(slots):
             heads(s, pair)
-    src = [far_grad.at[pl.ds(2 * d, 2)] for d in range(4)]
-    dst = [back.at[d] for d in range(4)]
+    returns = [
+        ([far_grad.at[2 * d + i] for d in range(4)], [back.at[d, i] for d in range(4)], *behind[i])
+        for i in range(2)
+    ]
     chain = sums()
-    next(chain)
-    terms()
-    for at in range(2, 7):
+    for at in range(1, 7):
         next(chain)
-        if at == RETURN_AT:
-            exchange_start(here, src, dst, *behind)
-        if at == RETURN_AT + 1:
-            exchange_relay(here, src, dst, *behind)
-    exchange_finish(here, src, dst, *behind)
+        if at == 1:
+            terms()
+        for i in range(2):
+            if at == RETURN_AT[i]:
+                exchange_start(here, *returns[i])
+            if at == RETURN_AT[i] + 1:
+                exchange_relay(here, *returns[i])
+    for i in range(2):
+        exchange_finish(here, *returns[i])
     acc = own_grad[...]
     for d in range(4):
         acc = acc + back[d].astype(F32)
@@ -449,8 +456,9 @@
             dma((3,)), dma((3,)),
             dma((3, 3)), dma((3, 3)),
             dma((3, 4)), dma((3, 4)),
-            *EXCHANGE_SCRATCH,
-            *EXCHANGE_SCRATCH,
+            *exchange_scratch(64),
+            *exchange_scratch(32),
+            *exchange_scratch(32),
         ],
         compiler_params=pltpu.CompilerParams(
             collective_id=0, has_side_effects=True, vmem_limit_bytes=VMEM_LIMIT

time: 90.3 us -> 88.2 us (0.977)
  Pallas kernels: 88.8 us -> 86.7 us
    pallas_call x1, Pallas kernels: 86.4 us -> 84.3 us  [layer(): pl.pallas_call(layer_kernel, out_shape=[jax.ShapeDtypeStruct((slots, poin...]
where the time goes in v6:
time: 88.2 us; the launch traced here: 88 us
  Pallas kernels  86.7 us (98%)
  between operations  1.29 us (1%)
    pallas_call x1, Pallas kernels, layer(): pl.pallas_call(layer_kernel, out_shape=[jax.ShapeDtypeStruct((slots, poin...  84.3 us
    pallas_call x1, Pallas kernels, finish(): pl.pallas_call(finish_kernel, out_shape=[jax.ShapeDtypeStruct(mixed.shape...  2.44 us

profile of v6, /device:TPU:1, one launch (start us, length us, event | category | flops | bytes accessed | tf_op | source)
XLA Modules:
  0.0 88.0 jit_solution(8574154479484506574)
XLA Ops:
  1.3 84.3 %layer.1 = (bf16[2,128,512]{2,1,0:T(8,128)(2,1)}, bf16[2,128,512]{2,1,0:T(8,128)(2,1)}, bf16[3,512,512]{2,1,0:T(8,128)(2,1)}) custom-call(s32[1,1]{1,0:T(1,128)S(6)} %copy.14.patch_count, s32[1,1,2]{2,1,0:T(1,128)} %point_count.1, s32[1,1,2,3]{3,2,1,0:T(2,128)} %neighbours.1, s32[1,1,2,3]{3,2,1,0:T(2,128)} %neighbour_points.1, bf16[2,128,512]{2,1,0:T(8,128)(2,1)} %bitcast.4, ...), custom_call_target="tpu_custom_call" | custom-call | tf_op jit(solution)/shard_map/layer/pallas_call | solution.py:426
  85.6 2.4 %finish.1 = (bf16[2,128,512]{2,1,0:T(8,128)(2,1)}, bf16[2,128,512]{2,1,0:T(8,128)(2,1)}, bf16[512,512]{1,0:T(8,128)(2,1)}, bf16[512,512]{1,0:T(8,128)(2,1)}, bf16[512,512]{1,0:T(8,128)(2,1)}) custom-call(bf16[2,128,512]{2,1,0:T(8,128)(2,1)} %get-tuple-element.13.mixed, bf16[2,128,512]{2,1,0:T(8,128)(2,1)} %get-tuple-element.14.feat_grad, ...), custom_call_target="tpu_custom_call" | custom-call | tf_op jit(solution)/shard_map/finish/pallas_call | solution.py:496

commit v7 on v6

--- a/solution.py
+++ b/solution.py
@@ -83,7 +83,7 @@
 
 def quarter(ref, p):
     if len(ref.shape) == 2:
-        return ref.at[pl.ds(p * 32, 32)]
+        return ref.at[pl.ds(p * (ref.shape[0] // 4), ref.shape[0] // 4)]
     return ref.at[p // 2, pl.ds(p % 2 * 64, 64)]
 
 
@@ -151,7 +151,7 @@
     return jnp.where(even & (code >= 2) & (code < 6), swapped, code)
 
 
-RETURN_AT = (2, 3)
+RETURN_AT = (2, 2, 3, 4)
 
 
 def layer_kernel(
@@ -182,7 +182,7 @@
     planes = [[moved(**{u: i, v: j}) for i, j in steps] for _, u, v in axes]
     deep = [moved(zh=k) for k in range(1, 4)]
     pieces = [(p, k) for k in range(4) for p in range(3)]
-    ahead, *behind = (scratch[i : i + 6] for i in (0, 6, 12))
+    ahead, *behind = (scratch[i : i + 6] for i in range(0, 30, 6))
 
     started = []
     for n, (src, dst) in enumerate(
@@ -388,21 +388,27 @@
     for pair in range(4):
         for s in range(slots):
             heads(s, pair)
-    returns = [
-        ([far_grad.at[2 * d + i] for d in range(4)], [back.at[d, i] for d in range(4)], *behind[i])
-        for i in range(2)
-    ]
+    returns = []
+    for i in range(4):
+        part = pl.ds(i % 2 * 64, 64)
+        returns.append(
+            (
+                [far_grad.at[2 * d + i // 2, part] for d in range(4)],
+                [back.at[d, i // 2, part] for d in range(4)],
+                *behind[i],
+            )
+        )
     chain = sums()
     for at in range(1, 7):
         next(chain)
         if at == 1:
             terms()
-        for i in range(2):
+        for i in range(4):
             if at == RETURN_AT[i]:
                 exchange_start(here, *returns[i])
             if at == RETURN_AT[i] + 1:
                 exchange_relay(here, *returns[i])
-    for i in range(2):
+    for i in range(4):
         exchange_finish(here, *returns[i])
     acc = own_grad[...]
     for d in range(4):
@@ -457,8 +463,10 @@
             dma((3, 3)), dma((3, 3)),
             dma((3, 4)), dma((3, 4)),
             *exchange_scratch(64),
-            *exchange_scratch(32),
-            *exchange_scratch(32),
+            *exchange_scratch(16),
+            *exchange_scratch(16),
+            *exchange_scratch(16),
+            *exchange_scratch(16),
         ],
         compiler_params=pltpu.CompilerParams(
             collective_id=0, has_side_effects=True, vmem_limit_bytes=VMEM_LIMIT

time: 88.2 us -> 86.9 us (0.985)
  Pallas kernels: 86.7 us -> 85.5 us
    pallas_call x1, Pallas kernels: 84.3 us -> 83 us  [layer(): pl.pallas_call(layer_kernel, out_shape=[jax.ShapeDtypeStruct((slots, poin...]
where the time goes in v7:
time: 86.9 us; the launch traced here: 86.8 us
  Pallas kernels  85.5 us (98%)
  between operations  1.29 us (1%)
    pallas_call x1, Pallas kernels, layer(): pl.pallas_call(layer_kernel, out_shape=[jax.ShapeDtypeStruct((slots, poin...  83 us
    pallas_call x1, Pallas kernels, finish(): pl.pallas_call(finish_kernel, out_shape=[jax.ShapeDtypeStruct(mixed.shape...  2.44 us

profile of v7, /device:TPU:1, one launch (start us, length us, event | category | flops | bytes accessed | tf_op | source)
XLA Modules:
  0.0 86.8 jit_solution(7122819346458519884)
XLA Ops:
  1.3 83.0 %layer.1 = (bf16[2,128,512]{2,1,0:T(8,128)(2,1)}, bf16[2,128,512]{2,1,0:T(8,128)(2,1)}, bf16[3,512,512]{2,1,0:T(8,128)(2,1)}) custom-call(s32[1,1]{1,0:T(1,128)S(6)} %copy.14.patch_count, s32[1,1,2]{2,1,0:T(1,128)} %point_count.1, s32[1,1,2,3]{3,2,1,0:T(2,128)} %neighbours.1, s32[1,1,2,3]{3,2,1,0:T(2,128)} %neighbour_points.1, bf16[2,128,512]{2,1,0:T(8,128)(2,1)} %bitcast.4, ...), custom_call_target="tpu_custom_call" | custom-call | tf_op jit(solution)/shard_map/layer/pallas_call | solution.py:432
  84.3 2.4 %finish.1 = (bf16[2,128,512]{2,1,0:T(8,128)(2,1)}, bf16[2,128,512]{2,1,0:T(8,128)(2,1)}, bf16[512,512]{1,0:T(8,128)(2,1)}, bf16[512,512]{1,0:T(8,128)(2,1)}, bf16[512,512]{1,0:T(8,128)(2,1)}) custom-call(bf16[2,128,512]{2,1,0:T(8,128)(2,1)} %get-tuple-element.13.mixed, bf16[2,128,512]{2,1,0:T(8,128)(2,1)} %get-tuple-element.14.feat_grad, ...), custom_call_target="tpu_custom_call" | custom-call | tf_op jit(solution)/shard_map/finish/pallas_call | solution.py:504

commit v8 on v7

--- a/solution.py
+++ b/solution.py
@@ -67,7 +67,7 @@
 
 def greet(here, peers):
     barrier = pltpu.get_barrier_semaphore()
-    peers = [here.partner, here.down, here.up, *peers]
+    peers = [*peers, here.down, here.up, here.partner]
     signal(peers)
 
     @pl.when(here.edge)
@@ -200,7 +200,7 @@
         moved(**{u: i, v: j}) for u, v in (("x", "y"), ("x", "zl"), ("y", "zl"))
         for i in range(1, 4) for j in range(1, 4)
     ]
-    greet(here, [*lines[0], *lines[1], *lines[2], *deep, *crosswise])
+    greet(here, [*deep[1:2], *deep[0:1], *deep[2:], *reversed(crosswise), *lines[0], *lines[1], *lines[2]])
     src = [feats] * 4
     dst = [table.at[pl.ds(2 + 2 * d, 2)] for d in range(4)]
     exchange_start(here, src, dst, *ahead)

time: 86.9 us -> 86.7 us (level)
  no operation moved by 1% of the time
where the time goes in v8:
time: 86.7 us; the launch traced here: 86.5 us
  Pallas kernels  85.2 us (98%)
  between operations  1.29 us (1%)
    pallas_call x1, Pallas kernels, layer(): pl.pallas_call(layer_kernel, out_shape=[jax.ShapeDtypeStruct((slots, poin...  82.8 us
    pallas_call x1, Pallas kernels, finish(): pl.pallas_call(finish_kernel, out_shape=[jax.ShapeDtypeStruct(mixed.shape...  2.44 us

profile of v8, /device:TPU:1, one launch (start us, length us, event | category | flops | bytes accessed | tf_op | source)
XLA Modules:
  0.0 86.5 jit_solution(10916884011009783847)
XLA Ops:
  1.3 82.8 %layer.1 = (bf16[2,128,512]{2,1,0:T(8,128)(2,1)}, bf16[2,128,512]{2,1,0:T(8,128)(2,1)}, bf16[3,512,512]{2,1,0:T(8,128)(2,1)}) custom-call(s32[1,1]{1,0:T(1,128)S(6)} %copy.14.patch_count, s32[1,1,2]{2,1,0:T(1,128)} %point_count.1, s32[1,1,2,3]{3,2,1,0:T(2,128)} %neighbours.1, s32[1,1,2,3]{3,2,1,0:T(2,128)} %neighbour_points.1, bf16[2,128,512]{2,1,0:T(8,128)(2,1)} %bitcast.4, ...), custom_call_target="tpu_custom_call" | custom-call | tf_op jit(solution)/shard_map/layer/pallas_call | solution.py:432
  84.1 2.4 %finish.1 = (bf16[2,128,512]{2,1,0:T(8,128)(2,1)}, bf16[2,128,512]{2,1,0:T(8,128)(2,1)}, bf16[512,512]{1,0:T(8,128)(2,1)}, bf16[512,512]{1,0:T(8,128)(2,1)}, bf16[512,512]{1,0:T(8,128)(2,1)}) custom-call(bf16[2,128,512]{2,1,0:T(8,128)(2,1)} %get-tuple-element.13.mixed, bf16[2,128,512]{2,1,0:T(8,128)(2,1)} %get-tuple-element.14.feat_grad, ...), custom_call_target="tpu_custom_call" | custom-call | tf_op jit(solution)/shard_map/finish/pallas_call | solution.py:504
